TPU v7x, 32 devices: a whole 2x2x4 slice. The times are simulated.
32 devices in a mesh: dp: 8 (over y, x, core), tensor: 4 (over z).
Axes of the slice: x: 2, y: 2, z: 4, core: 2. Of those that a mesh axis runs over, the one named last changes fastest.
Arguments:
- tokens: bfloat16 [8192, 768], P(('dp', 'tensor')), may hold values from -6 to 6
- cotangent: bfloat16 [8192, 768], P(('dp', 'tensor')), may hold values from -6 to 6
- norm_gain: float32 [2, 2, 768], replicated, may hold values from 0.5 to 1.5
- norm_shift: float32 [2, 2, 768], replicated, may hold values from -3 to 3
- w_qkv: bfloat16 [2, 768, 3, 768], P(None, None, None, 'tensor'), may hold values from -0.3125 to 0.3125
- b_qkv: float32 [2, 3, 768], P(None, None, 'tensor'), may hold values from -3 to 3
- w_out: bfloat16 [2, 768, 768], P(None, 'tensor'), may hold values from -2 to 2
- b_out: float32 [2, 768], replicated, may hold values from -3 to 3
- w_in: bfloat16 [2, 768, 3072], P(None, None, 'tensor'), may hold values from -0.21875 to 0.21875
- b_in: float32 [2, 3072], P(None, 'tensor'), may hold values from -3 to 3
- w_down: bfloat16 [2, 3072, 768], P(None, 'tensor'), may hold values from -0.109375 to 0.109375
- b_down: float32 [2, 768], replicated, may hold values from -3 to 3
Outputs:
- result: float32 [8192, 768], P(('dp', 'tensor'))
- grad_tokens: float32 [8192, 768], P(('dp', 'tensor'))
- grad_norm_gain: float32 [2, 2, 768], replicated
- grad_norm_shift: float32 [2, 2, 768], replicated
- grad_w_qkv: float32 [2, 768, 3, 768], P(None, None, None, 'tensor')
- grad_b_qkv: float32 [2, 3, 768], P(None, None, 'tensor')
- grad_w_out: float32 [2, 768, 768], P(None, 'tensor')
- grad_b_out: float32 [2, 768], replicated
- grad_w_in: float32 [2, 768, 3072], P(None, None, 'tensor')
- grad_b_in: float32 [2, 3072], P(None, 'tensor')
- grad_w_down: float32 [2, 3072, 768], P(None, 'tensor')
- grad_b_down: float32 [2, 768], replicated
All inputs are finite; a program needn't handle non-finite values.
Results may differ from a plain program's by a relative error of at most 0.03.
The roundings to bfloat16 on the way count: a program that leaves them out, or rounds other values in their place, can miss the bound.
Values may be sent and summed in bfloat16 or wider, within the bound.
No kernel may reach another device: no remote copies, remote signals or barrier semaphores. Data moves between devices by JAX's collectives and lax.ppermute only.
A program may use at most 128 MiB of HBM per device.

v0:
```python
import math

import jax
import jax.numpy as jnp
from jax import lax
from jax.sharding import PartitionSpec as P

HD = 64
ROT = 16
LEN = 1024


epsilon = 1e-05


def layer_norm(rows, gain, shift):
    centre = rows - jnp.mean(rows, axis=-1, keepdims=True)
    spread = jnp.mean(centre * centre, axis=-1, keepdims=True)
    return centre * lax.rsqrt(spread + epsilon) * gain + shift


def both_norms(rows, gains, shifts):
    return (layer_norm(rows, gains[0], shifts[0]), layer_norm(rows, gains[1], shifts[1]))


def rotary_tables(count):
    half = ROT // 2
    places = (jnp.arange(count, dtype=jnp.int32) % LEN).astype(jnp.float32)
    freqs = jnp.exp(jnp.arange(half, dtype=jnp.float32) * (-2.0 * math.log(10000.0) / ROT))
    angles = places[:, None] * freqs[None, :]
    return (jnp.cos(angles)[:, None, :], jnp.sin(angles)[:, None, :])


def rotate(values, cosine, sine):
    half = ROT // 2
    first = values[..., :half]
    second = values[..., half:ROT]
    return jnp.concatenate(
        [first * cosine - second * sine, second * cosine + first * sine, values[..., ROT:]], axis=-1
    )


def rotate_back(grads, cosine, sine):
    half = ROT // 2
    first = grads[..., :half]
    second = grads[..., half:ROT]
    return jnp.concatenate(
        [first * cosine + second * sine, second * cosine - first * sine, grads[..., ROT:]], axis=-1
    )


def gelu_exact(values):
    return jax.nn.gelu(values, approximate=False)


def block_scores(query, key, block_index, block):
    first_row = block_index * block
    seq_start = first_row // LEN * LEN
    q_rows = lax.dynamic_slice_in_dim(query, first_row, block, 0)
    scores = jnp.einsum("qhd,khd->hqk", q_rows, key, preferred_element_type=jnp.float32) * HD ** (
        -0.5
    )
    places = first_row % LEN + jnp.arange(block, dtype=jnp.int32)
    causal = jnp.arange(LEN, dtype=jnp.int32)[None, :] <= places[:, None]
    return (jnp.where(causal[None], scores, -1e30), q_rows, key, seq_start)


def attend_forward(query, key, value, block):
    count = query.shape[0]

    def one_block(block_index):
        scores, q_rows, k_rows, seq_start = block_scores(query, key, block_index, block)
        top = jnp.max(scores, axis=-1, keepdims=True)
        weights = jnp.exp(scores - top)
        total = jnp.sum(weights, axis=-1, keepdims=True)
        probs = (weights / total).astype(jnp.bfloat16)
        mixed = jnp.einsum("hqk,khd->qhd", probs, value, preferred_element_type=jnp.float32).astype(
            jnp.bfloat16
        )
        return (mixed, (top + jnp.log(total))[..., 0])

    mixed, log_total = lax.map(one_block, jnp.arange(count // block, dtype=jnp.int32))
    return (mixed.reshape(count, query.shape[1], query.shape[2]), log_total)


def attend_backward(query, key, value, log_total, grad_mixed, block):
    count = query.shape[0]
    heads_here = query.shape[1]
    per_seq = LEN // block

    def one_block(block_index):
        scores, q_rows, k_rows, seq_start = block_scores(query, key, block_index, block)
        g_rows = lax.dynamic_slice_in_dim(grad_mixed, block_index * block, block, 0)
        probs = jnp.exp(scores - log_total[block_index][:, :, None])
        low_probs = probs.astype(jnp.bfloat16)
        grad_value = jnp.einsum(
            "hqk,qhd->khd", low_probs, g_rows, preferred_element_type=jnp.float32
        )
        grad_probs = jnp.einsum("qhd,khd->hqk", g_rows, value, preferred_element_type=jnp.float32)
        grad_scores = probs * (grad_probs - jnp.sum(probs * grad_probs, axis=-1, keepdims=True))
        low_grad = grad_scores.astype(jnp.bfloat16)
        grad_query = jnp.einsum(
            "hqk,khd->qhd", low_grad, k_rows, preferred_element_type=jnp.float32
        ) * HD ** (-0.5)
        grad_key = jnp.einsum(
            "hqk,qhd->khd", low_grad, q_rows, preferred_element_type=jnp.float32
        ) * HD ** (-0.5)
        return (grad_query, grad_key, grad_value)

    grad_query, grad_key, grad_value = lax.map(
        one_block, jnp.arange(count // block, dtype=jnp.int32)
    )
    grad_query = grad_query.reshape(count, heads_here, HD)
    grad_key = (
        grad_key.reshape(count // LEN, per_seq, LEN, heads_here, HD)
        .sum(axis=1)
        .reshape(count, heads_here, HD)
    )
    grad_value = (
        grad_value.reshape(count // LEN, per_seq, LEN, heads_here, HD)
        .sum(axis=1)
        .reshape(count, heads_here, HD)
    )
    return (grad_query, grad_key, grad_value)


def body(
    tokens, cotangent, norm_gain, norm_shift, w_qkv, b_qkv, w_out, b_out, w_in, b_in, w_down, b_down
):
    layers = w_qkv.shape[0]
    rows = tokens.shape[0]
    heads_here = w_qkv.shape[3] // HD
    count = rows * lax.axis_size("tensor")
    block = min(512, LEN)
    cosine, sine = rotary_tables(count)
    stream = tokens.astype(jnp.float32)
    kept = []
    for layer_index in range(layers):
        gains = norm_gain[layer_index]
        shifts = norm_shift[layer_index]
        first_norm, second_norm = both_norms(stream, gains, shifts)
        attn_in, mlp_in = (
            lax.all_gather(first_norm.astype(jnp.bfloat16), "tensor", axis=0, tiled=True),
            lax.all_gather(second_norm.astype(jnp.bfloat16), "tensor", axis=0, tiled=True),
        )
        norm_keep = None
        projected = (
            jnp.einsum(
                "td,dcf->tcf", attn_in, w_qkv[layer_index], preferred_element_type=jnp.float32
            )
            + b_qkv[layer_index]
        )
        split = projected.reshape(count, 3, heads_here, HD)
        query = rotate(split[:, 0], cosine, sine).astype(jnp.bfloat16)
        key = rotate(split[:, 1], cosine, sine).astype(jnp.bfloat16)
        value = split[:, 2].astype(jnp.bfloat16)
        attended, log_total = attend_forward(query, key, value, block)
        mixed = attended.reshape(count, heads_here * HD)
        hidden_pre = (
            jnp.dot(mlp_in, w_in[layer_index], preferred_element_type=jnp.float32)
            + b_in[layer_index]
        )
        hidden = gelu_exact(hidden_pre).astype(jnp.bfloat16)

        def branch_term(
            start,
            size,
            mixed=mixed,
            hidden=hidden,
            out_weight=w_out[layer_index],
            down_weight=w_down[layer_index],
        ):
            return jnp.dot(mixed, out_weight, preferred_element_type=jnp.float32) + jnp.dot(
                hidden, down_weight, preferred_element_type=jnp.float32
            )

        branch = lax.psum_scatter(
            branch_term(jnp.int32(0), rows * lax.axis_size("tensor")),
            "tensor",
            scatter_dimension=0,
            tiled=True,
        )
        kept.append(
            (
                stream,
                attn_in,
                mlp_in,
                query,
                key,
                value,
                log_total,
                mixed,
                hidden_pre,
                hidden,
                norm_keep,
            )
        )
        stream = stream + branch + b_out[layer_index] + b_down[layer_index]
    grad_stream = cotangent.astype(jnp.float32)
    packs = [None] * layers
    gain_grads = [None] * layers
    shift_grads = [None] * layers
    bias_grads = [None] * layers
    for layer_index in reversed(range(layers)):
        (
            stream_in,
            attn_in,
            mlp_in,
            query,
            key,
            value,
            log_total,
            mixed,
            hidden_pre,
            hidden,
            norm_keep,
        ) = kept[layer_index]
        gains = norm_gain[layer_index]
        grad_low = grad_stream.astype(jnp.bfloat16)
        bias_grads[layer_index] = jnp.sum(grad_low.astype(jnp.float32), axis=0)
        grad_all = lax.all_gather(grad_low, "tensor", axis=0, tiled=True)
        grad_w_out = jnp.einsum("tf,td->fd", mixed, grad_all, preferred_element_type=jnp.float32)
        grad_w_down = jnp.einsum("tf,td->fd", hidden, grad_all, preferred_element_type=jnp.float32)
        grad_mixed = jnp.einsum(
            "td,fd->tf", grad_all, w_out[layer_index], preferred_element_type=jnp.float32
        ).astype(jnp.bfloat16)
        grad_hidden = jnp.einsum(
            "td,fd->tf", grad_all, w_down[layer_index], preferred_element_type=jnp.float32
        )
        unused_value, gelu_pull = jax.vjp(gelu_exact, hidden_pre)
        grad_pre = gelu_pull(grad_hidden)[0].astype(jnp.bfloat16)
        grad_w_in = jnp.einsum("td,tf->df", mlp_in, grad_pre, preferred_element_type=jnp.float32)
        grad_b_in = jnp.sum(grad_pre.astype(jnp.float32), axis=0)
        grad_mlp_in = jnp.einsum(
            "tf,df->td", grad_pre, w_in[layer_index], preferred_element_type=jnp.float32
        )
        grad_query, grad_key, grad_value = attend_backward(
            query, key, value, log_total, grad_mixed.reshape(count, heads_here, HD), block
        )
        grad_projected = jnp.stack(
            [
                rotate_back(grad_query, cosine, sine),
                rotate_back(grad_key, cosine, sine),
                grad_value,
            ],
            axis=1,
        )
        grad_projected = grad_projected.reshape(count, 3, heads_here * HD).astype(jnp.bfloat16)
        grad_w_qkv = jnp.einsum(
            "td,tcf->dcf", attn_in, grad_projected, preferred_element_type=jnp.float32
        )
        grad_b_qkv = jnp.sum(grad_projected.astype(jnp.float32), axis=0)
        grad_attn_in = jnp.einsum(
            "tcf,dcf->td", grad_projected, w_qkv[layer_index], preferred_element_type=jnp.float32
        )
        grad_first, grad_second = (
            lax.psum_scatter(
                grad_attn_in.astype(jnp.bfloat16), "tensor", scatter_dimension=0, tiled=True
            ).astype(jnp.float32),
            lax.psum_scatter(
                grad_mlp_in.astype(jnp.bfloat16), "tensor", scatter_dimension=0, tiled=True
            ).astype(jnp.float32),
        )
        unused_norms, norm_pull = jax.vjp(both_norms, stream_in, gains, norm_shift[layer_index])
        grad_rows, grad_gain, grad_shift = norm_pull((grad_first, grad_second))
        gain_grads[layer_index] = grad_gain
        shift_grads[layer_index] = grad_shift
        grad_stream = grad_stream + grad_rows
        layer_pack = (grad_w_qkv, grad_b_qkv, grad_w_out, grad_w_in, grad_b_in, grad_w_down)
        packs[layer_index] = layer_pack
    stacked = tuple((jnp.stack([pack[member] for pack in packs]) for member in range(6)))
    stacked = lax.psum(
        (stacked[0], stacked[1], stacked[2], stacked[3], stacked[4], stacked[5]), "dp"
    )
    summed_gain, summed_shift, summed_bias = lax.psum(
        (jnp.stack(gain_grads), jnp.stack(shift_grads), jnp.stack(bias_grads)), ("dp", "tensor")
    )
    return (
        stream,
        grad_stream,
        summed_gain,
        summed_shift,
        stacked[0],
        stacked[1],
        stacked[2],
        summed_bias,
        stacked[3],
        stacked[4],
        stacked[5],
        summed_bias,
    )


def solution(mesh):
    in_specs = (
        P(("dp", "tensor"), None),
        P(("dp", "tensor"), None),
        P(),
        P(),
        P(None, None, None, "tensor"),
        P(None, None, "tensor"),
        P(None, "tensor", None),
        P(),
        P(None, None, "tensor"),
        P(None, "tensor"),
        P(None, "tensor", None),
        P(),
    )
    out_specs = (
        P(("dp", "tensor"), None),
        P(("dp", "tensor"), None),
        P(),
        P(),
        P(None, None, None, "tensor"),
        P(None, None, "tensor"),
        P(None, "tensor", None),
        P(),
        P(None, None, "tensor"),
        P(None, "tensor"),
        P(None, "tensor", None),
        P(),
    )
    return jax.shard_map(body, mesh=mesh, in_specs=in_specs, out_specs=out_specs, check_vma=False)
```

profile of v0, /device:TPU:0, one launch (start us, length us, event | category | flops | bytes accessed | tf_op | source)
XLA Modules:
  0.0 885.0 jit_solution(8449013625506411080)
XLA Ops:
  11.7 2.2 fusion.129
  16.8 37.0 %all-gather.7.cloned.1.call-done = bf16[1024,768]{1,0:T(8,128)(2,1)} async-done(((bf16[256,768]{1,0:T(8,128)(2,1)}), bf16[1024,768]{1,0:T(8,128)(2,1)}) %all-gather.7.cloned.1.call-update) | async-done | bytes 1572880 | tf_op jit(solution)/shard_map/all_gather | solution.py:143
  53.9 2.7 fusion.169
  57.3 14.2 %while.60 = (s32[]{:T(128)}, bf16[2,512,3,64]{1,3,2,0:T(8,128)(2,1)S(1)}, f32[2,3,512]{2,1,0:T(4,128)S(1)}, s32[2]{0:T(128)S(1)}, bf16[1024,3,64]{0,2,1:T(8,128)...) while((s32[]{:T(128)}, ...), condition=%wide.region_5.6_spmd, body=%wide.region_2.0_spmd.sunk | while | flops 422149120 | bytes 22214956 | solution.py:82
  62.1 2.2 fusion.261
  69.2 2.2 fusion.261
  72.0 20.1 %all-gather.9.cloned.1.call-done = bf16[1024,768]{1,0:T(8,128)(2,1)} async-done(((bf16[256,768]{1,0:T(8,128)(2,1)}), bf16[1024,768]{1,0:T(8,128)(2,1)}) %all-gather.9.cloned.1.call-update) | async-done | bytes 1572880 | tf_op jit(solution)/shard_map/all_gather | solution.py:144
  92.1 11.5 %multiply_convert_fusion.3 = (bf16[1024,768]{1,0:T(8,128)(2,1)S(1)}, f32[1024,768]{1,0:T(8,128)}, f32[1024,768]{1,0:T(8,128)}) fusion(f32[768]{0:T(1024)S(1)} %get-tuple-element.505, bf16[1024,768]{1,0:T(8,128)(2,1)} %all-gather.9.cloned.1.call-done, bf16[2,768,768]{2,1,0:T(8,128)(2,1)} %param.28), kind=kOutput, calls=%fused_computation.116 | convolution fusion | flops 1259864064 | bytes 10619904 | tf_op jit(solution)/shard_map/dot_general | solution.py:160
  105.2 2.3 convolution_add_fusion.1
  109.0 57.8 %reduce-scatter.7.cloned.1.call-done = f32[256,768]{1,0:T(8,128)} async-done(((f32[1024,768]{1,0:T(8,128)}), f32[256,768]{1,0:T(8,128)}) %reduce-scatter.7.cloned.1.call-update) | async-done | bytes 786448 | tf_op jit(solution)/shard_map/reduce_scatter | solution.py:177
  170.9 34.5 %all-gather.15.cloned.1.call-done = bf16[1024,768]{1,0:T(8,128)(2,1)} async-done(((bf16[256,768]{1,0:T(8,128)(2,1)}), bf16[1024,768]{1,0:T(8,128)(2,1)}) %all-gather.15.cloned.1.call-update) | async-done | bytes 1572880 | tf_op jit(solution)/shard_map/all_gather | solution.py:221
  205.4 2.1 convolution_convert_fusion.3
  207.5 35.9 %all-gather.11.cloned.1.call-done = bf16[1024,768]{1,0:T(8,128)(2,1)} async-done(((bf16[256,768]{1,0:T(8,128)(2,1)}), bf16[1024,768]{1,0:T(8,128)(2,1)}) %all-gather.11.cloned.1.call-update) | async-done | bytes 1572880 | tf_op jit(solution)/shard_map/all_gather | solution.py:143
  243.4 2.5 fusion.170
  246.5 34.9 %all-gather.13.cloned.1.call-done = bf16[1024,768]{1,0:T(8,128)(2,1)} async-done(((bf16[256,768]{1,0:T(8,128)(2,1)}), bf16[1024,768]{1,0:T(8,128)(2,1)}) %all-gather.13.cloned.1.call-update) | async-done | bytes 1572880 | tf_op jit(solution)/shard_map/all_gather | solution.py:144
  281.4 22.3 %multiply_convert_fusion.2 = (bf16[1024,768]{1,0:T(8,128)(2,1)}, f32[1024,768]{1,0:T(8,128)S(1)}, f32[1024,768]{1,0:T(8,128)S(1)}) fusion(f32[768]{0:T(1024)S(1)} %get-tuple-element.504, bf16[1024,768]{1,0:T(8,128)(2,1)} %all-gather.13.cloned.1.call-done, bf16[2,768,768]{2,1,0:T(8,128)(2,1)} %param.28), kind=kOutput, calls=%fused_computation.103 | convolution fusion | flops 1259864064 | bytes 10619904 | tf_op jit(solution)/shard_map/dot_general | solution.py:160
  303.6 2.8 convert_reduce_fusion
  307.6 2.6 convolution_convert_fusion.1
  310.7 14.2 %while.61 = (s32[]{:T(128)}, bf16[2,512,3,64]{1,3,2,0:T(8,128)(2,1)S(1)}, f32[2,3,512]{2,1,0:T(4,128)S(1)}, s32[2]{0:T(128)S(1)}, bf16[1024,3,64]{0,2,1:T(8,128)...) while((s32[]{:T(128)}, ...), condition=%wide.region_12.13_spmd, body=%wide.region_9.12_spmd.sunk | while | flops 422149120 | bytes 22214956 | solution.py:82
  315.6 2.2 fusion.266
  322.7 2.2 fusion.266
  328.7 66.5 %while.62 = (s32[]{:T(128)}, f32[2,512,3,64]{1,0,3,2:T(2,128)}, f32[2,1024,3,64]{1,3,2,0:T(8,128)}, f32[2,1024,3,64]{1,3,2,0:T(8,128)}, s32[2]{0:T(128)S(1)}, /*...) while((s32[]{:T(128)}, f32[2,512,3,64]{1,0,3,2:T(2,128)}, ...), condition=%wide.region_19.20_spmd, body=%wide.region_17.19_spmd.sunk | while | flops 1031044096 | bytes 100027168 | solution.py:110
  330.1 3.7 fusion.276
  336.1 4.8 multiply_reduce_fusion.5
  345.1 8.1 dynamic_update_slice.88
  353.2 2.6 fusion.278
  355.9 4.8 fusion.279
  363.3 3.7 fusion.276
  369.4 4.8 multiply_reduce_fusion.5
  378.3 8.1 dynamic_update_slice.88
  386.4 2.6 fusion.278
  389.0 4.8 fusion.279
  401.9 2.6 bitcast_convert_fusion.1
  406.4 2.9 fusion.92
  409.2 2.3 convolution_add_fusion
  411.7 27.2 %reduce-scatter.13.cloned.1.call-done = bf16[256,768]{1,0:T(8,128)(2,1)} async-done(((bf16[1024,768]{1,0:T(8,128)(2,1)}), bf16[256,768]{1,0:T(8,128)(2,1)}) %reduce-scatter.13.cloned.1.call-update) | async-done | bytes 393232 | tf_op jit(solution)/shard_map/reduce_scatter | solution.py:257
  440.6 2.5 fusion.137
  443.2 57.8 %reduce-scatter.9.cloned.1.call-done = f32[256,768]{1,0:T(8,128)} async-done(((f32[1024,768]{1,0:T(8,128)}), f32[256,768]{1,0:T(8,128)}) %reduce-scatter.9.cloned.1.call-update) | async-done | bytes 786448 | tf_op jit(solution)/shard_map/reduce_scatter | solution.py:177
  501.0 3.7 convert_reduce_fusion.10
  504.8 37.2 %all-gather.17.cloned.1.call-done = bf16[1024,768]{1,0:T(8,128)(2,1)} async-done(((bf16[256,768]{1,0:T(8,128)(2,1)}), bf16[1024,768]{1,0:T(8,128)(2,1)}) %all-gather.17.cloned.1.call-update) | async-done | bytes 1572880 | tf_op jit(solution)/shard_map/all_gather | solution.py:221
  542.0 6.5 convert_reduce_fusion.1
  549.7 2.6 convolution_convert_fusion
  556.8 69.8 %while.63 = (s32[]{:T(128)}, f32[2,512,3,64]{1,0,3,2:T(2,128)}, f32[2,1024,3,64]{1,3,2,0:T(8,128)}, f32[2,1024,3,64]{1,3,2,0:T(8,128)}, s32[2]{0:T(128)S(1)}, /*...) while((s32[]{:T(128)}, f32[2,512,3,64]{1,0,3,2:T(2,128)}, ...), condition=%wide.region_30.31_spmd, body=%wide.region_28.30_spmd.sunk | while | flops 1031044096 | bytes 95210232 | solution.py:110
  558.4 4.6 fusion.289
  566.2 4.8 multiply_reduce_fusion.6
  575.2 8.0 dynamic_update_slice.91
  583.3 2.6 fusion.291
  585.9 4.8 fusion.292
  593.3 4.6 fusion.289
  601.1 4.8 multiply_reduce_fusion.6
  610.0 8.0 dynamic_update_slice.91
  618.0 2.6 fusion.291
  620.7 4.8 fusion.292
  632.8 2.6 bitcast_convert_fusion
  635.9 2.6 fusion.172
  649.4 2.5 pad_maximum_fusion
  653.3 2.5 pad_maximum_fusion.1
  656.7 24.5 %all-reduce.9 = (f32[2,3,192]{2,1,0:T(4,128)S(1)}, f32[2,768]{1,0:T(2,128)}) all-reduce(f32[2,3,192]{2,1,0:T(4,128)S(1)} %pad_maximum_fusion.16, f32[2,768]{1,0:T(2,128)S(1)} %pad_maximum_fusion.18), channel_id=1, replica_groups=mesh['dp'=8,'tensor'=4] {'dp'}, use_global_device_ids=true, to_apply=%region_49.50 | all-reduce | flops 2688 | bytes 21504 | tf_op jit(solution)/shard_map/psum | solution.py:272
  685.5 40.0 %all-reduce.8 = (f32[2,2,768]{2,1,0:T(2,128)}, f32[2,2,768]{2,1,0:T(2,128)}, f32[2,768]{1,0:T(2,128)S(1)}) all-reduce(f32[2,2,768]{2,1,0:T(2,128)S(1)} %pad_maximum_fusion.14, f32[2,2,768]{2,1,0:T(2,128)S(1)} %pad_maximum_fusion.15, f32[2,768]{1,0:T(2,128)S(1)} %pad_maximum_fusion.17), channel_id=1, replica_groups=mesh['dp'=8,'tensor'=4] {'dp','tensor'}, use_global_device_ids=true, to_apply=%region_40.41 | all-reduce | flops 7680 | bytes 61440 | tf_op jit(solution)/shard_map/psum | solution.py:275
  725.6 2.5 add_add_fusion.4
  728.1 138.0 %all-reduce.13.cloned.1.call-done = (f32[2,768,3,192]{1,3,2,0:T(8,128)}, f32[2,192,768]{2,1,0:T(8,128)}, f32[2,768,768]{2,1,0:T(8,128)}, f32[2,768,768]{2,1,0:T(8,128)}) async-done(((f32[2,768,3,192]{1,3,2,0:T(8,128)}, f32[2,192,768]{2,1,0:T(8,128)}, f32[2,768,768]{2,1,0:T(8,128)}, f32[2,768,768]{2,1,0:T(8,128)}), (f32[2,768,3,192]{1,3,2,0:T(8,128)}, f32[2,192,768]{2,1,0:T(8,128)}, ...) | async-done | bytes 14155792 | tf_op jit(solution)/shard_map/psum | solution.py:272
  866.7 4.6 copy.146
  872.3 2.4 copy.148
  875.9 2.2 copy.149
  (496 shorter events, 107.0 us)
Async XLA Ops:
  7.2 8.4 copy-start.37
  7.2 9.4 %copy-start.90 = (f32[2,3,192]{2,0,1:T(2,128)S(1)}, f32[2,3,192]{2,0,1:T(2,128)}, u32[]{:S(2)}) copy-start(f32[2,3,192]{2,0,1:T(2,128)} %param.25) | copy-start | bytes 13828
  7.2 46.7 %all-gather.7.cloned.1.call-start = ((), (), s32[]{:S(2)}) async-start(), calls=%async_computation.6 | async-start | bytes 1966080 | tf_op jit(solution)/shard_map/all_gather | solution.py:143
  8.5 48.1 %copy-start.69 = (f32[256]{0:T(256)}, f32[256]{0:T(256)S(1)}, u32[]{:S(2)}) copy-start(f32[256]{0:T(256)S(1)} %broadcast_multiply_fusion.1) | copy-start | bytes 3076
  10.3 46.4 %copy-start.73 = (f32[256]{0:T(256)}, f32[256]{0:T(256)S(1)}, u32[]{:S(2)}) copy-start(f32[256]{0:T(256)S(1)} %fusion.157) | copy-start | bytes 3076
  11.2 157.3 %copy-start.65 = (f32[768]{0:T(1024)}, f32[768]{0:T(1024)S(1)}, u32[]{:S(2)}) copy-start(f32[768]{0:T(1024)S(1)} %get-tuple-element.654) | copy-start | bytes 9220
  11.2 157.3 %copy-start.67 = (f32[768]{0:T(1024)}, f32[768]{0:T(1024)S(1)}, u32[]{:S(2)}) copy-start(f32[768]{0:T(1024)S(1)} %get-tuple-element.657) | copy-start | bytes 9220
  13.9 78.2 %all-gather.9.cloned.1.call-start = ((), (), s32[]{:S(2)}) async-start(), calls=%async_computation.7 | async-start | bytes 1966080 | tf_op jit(solution)/shard_map/all_gather | solution.py:144
  14.7 152.1 %reduce-scatter.7.cloned.1.call-start = ((), (), s32[]{:S(2)}) async-start(), calls=%async_computation.8 | async-start | bytes 3932160 | tf_op jit(solution)/shard_map/reduce_scatter | solution.py:177
  15.5 76.6 %copy-start.92 = (f32[768]{0:T(1024)}, f32[768]{0:T(1024)S(1)}, u32[]{:S(2)}) copy-start(f32[768]{0:T(1024)S(1)} %get-tuple-element.505) | copy-start | bytes 9220
  16.8 229.5 %copy-start.50 = (f32[1024,8]{0,1:T(8,128)}, f32[1024,8]{0,1:T(8,128)S(1)}, u32[]{:S(2)}) copy-start(f32[1024,8]{0,1:T(8,128)S(1)} %get-tuple-element.646) | copy-start | bytes 98308
  16.8 229.5 %copy-start.53 = (f32[1024,8]{0,1:T(8,128)}, f32[1024,8]{0,1:T(8,128)S(1)}, u32[]{:S(2)}) copy-start(f32[1024,8]{0,1:T(8,128)S(1)} %get-tuple-element.647) | copy-start | bytes 98308
  71.5 32.1 %copy-start.4 = (bf16[1024,3,64]{0,2,1:T(8,128)(2,1)}, bf16[1024,3,64]{0,2,1:T(8,128)(2,1)S(1)}, u32[]{:S(2)}) copy-start(bf16[1024,3,64]{0,2,1:T(8,128)(2,1)S(1)} %get-tuple-element.1108) | copy-start | bytes 1179652
  71.5 32.1 %copy-start.6 = (bf16[1024,3,64]{0,2,1:T(8,128)(2,1)}, bf16[1024,3,64]{0,2,1:T(8,128)(2,1)S(1)}, u32[]{:S(2)}) copy-start(bf16[1024,3,64]{0,2,1:T(8,128)(2,1)S(1)} %get-tuple-element.1110) | copy-start | bytes 1179652
  71.5 32.1 %copy-start.13 = (bf16[1024,3,64]{0,2,1:T(8,128)(2,1)}, bf16[1024,3,64]{0,2,1:T(8,128)(2,1)S(1)}, u32[]{:S(2)}) copy-start(bf16[1024,3,64]{0,2,1:T(8,128)(2,1)S(1)} %get-tuple-element.1116) | copy-start | bytes 1179652
  71.5 32.1 %copy-start.58 = (f32[2,3,512]{2,1,0:T(4,128)}, f32[2,3,512]{2,1,0:T(4,128)S(1)}, u32[]{:S(2)}) copy-start(f32[2,3,512]{2,1,0:T(4,128)S(1)} %get-tuple-element.1011) | copy-start | bytes 36868
  72.0 33.1 %copy-start.26 = (bf16[24,8,2,512]{3,1,2,0:T(8,128)(2,1)}, bf16[24,8,2,512]{3,1,2,0:T(8,128)(2,1)S(1)}, u32[]{:S(2)}) copy-start(bf16[24,8,2,512]{3,1,2,0:T(8,128)(2,1)S(1)} %copy.74) | copy-start | bytes 1179652
  92.1 11.5 %copy-start.96 = (bf16[2,768,768]{2,1,0:T(8,128)(2,1)S(1)}, bf16[2,768,768]{2,1,0:T(8,128)(2,1)}, u32[]{:S(2)}) copy-start(bf16[2,768,768]{2,1,0:T(8,128)(2,1)} %param.30) | copy-start | bytes 7077892
  107.5 59.3 %copy-start.11 = (bf16[256,768]{1,0:T(8,128)(2,1)S(1)}, bf16[256,768]{1,0:T(8,128)(2,1)}, u32[]{:S(2)}) copy-start(bf16[256,768]{1,0:T(8,128)(2,1)} %param.20) | copy-start | bytes 1179652
  107.5 97.9 %all-gather.15.cloned.1.call-start = ((), (), s32[]{:S(2)}) async-start(), calls=%async_computation.12 | async-start | bytes 1966080 | tf_op jit(solution)/shard_map/all_gather | solution.py:221
  108.1 135.3 %all-gather.11.cloned.1.call-start = ((), (), s32[]{:S(2)}) async-start(), calls=%async_computation.9 | async-start | bytes 1966080 | tf_op jit(solution)/shard_map/all_gather | solution.py:143
  168.2 77.7 %copy-start.71 = (f32[256]{0:T(256)}, f32[256]{0:T(256)S(1)}, u32[]{:S(2)}) copy-start(f32[256]{0:T(256)S(1)} %broadcast_multiply_fusion) | copy-start | bytes 3076
  168.4 77.5 %copy-start.86 = (f32[256]{0:T(256)}, f32[256]{0:T(256)S(1)}, u32[]{:S(2)}) copy-start(f32[256]{0:T(256)S(1)} %multiply_reduce_fusion.2) | copy-start | bytes 3076
  168.4 77.5 %copy-start.75 = (f32[256]{0:T(256)}, f32[256]{0:T(256)S(1)}, u32[]{:S(2)}) copy-start(f32[256]{0:T(256)S(1)} %fusion.158) | copy-start | bytes 3076
  170.2 111.1 %all-gather.13.cloned.1.call-start = ((), (), s32[]{:S(2)}) async-start(), calls=%async_computation.10 | async-start | bytes 1966080 | tf_op jit(solution)/shard_map/all_gather | solution.py:144
  170.8 240.9 %reduce-scatter.11.cloned.1.call-start = ((), (), s32[]{:S(2)}) async-start(), calls=%async_computation.13 | async-start | bytes 1966080 | tf_op jit(solution)/shard_map/reduce_scatter | solution.py:260
  281.3 22.3 %copy-start.40 = (bf16[1024,768]{1,0:T(8,128)(2,1)S(1)}, bf16[1024,768]{1,0:T(8,128)(2,1)}, u32[]{:S(2)}) copy-start(bf16[1024,768]{1,0:T(8,128)(2,1)} %all-gather.15.cloned.1.call-done) | copy-start | bytes 4718596
  281.4 22.3 %copy-start.97 = (bf16[2,768,768]{2,1,0:T(8,128)(2,1)S(1)}, bf16[2,768,768]{2,1,0:T(8,128)(2,1)}, u32[]{:S(2)}) copy-start(bf16[2,768,768]{2,1,0:T(8,128)(2,1)} %param.30) | copy-start | bytes 7077892
  310.1 128.7 %reduce-scatter.13.cloned.1.call-start = ((), (), s32[]{:S(2)}) async-start(), calls=%async_computation.14 | async-start | bytes 1966080 | tf_op jit(solution)/shard_map/reduce_scatter | solution.py:257
  328.7 7.0 copy-start.59
  328.7 7.4 copy-start.16
  328.7 7.4 copy-start.33
  361.9 7.0 copy-start.59
  361.9 7.4 copy-start.16
  361.9 7.4 copy-start.33
  404.6 96.4 %reduce-scatter.9.cloned.1.call-start = ((), (), s32[]{:S(2)}) async-start(), calls=%async_computation.11 | async-start | bytes 3932160 | tf_op jit(solution)/shard_map/reduce_scatter | solution.py:177
  411.5 27.3 %copy-start.10 = (f32[256,768]{1,0:T(8,128)S(1)}, f32[256,768]{1,0:T(8,128)}, u32[]{:S(2)}) copy-start(f32[256,768]{1,0:T(8,128)} %copy-done.9) | copy-start | bytes 2359300
  411.5 27.3 %copy-start.66 = (f32[768]{0:T(1024)S(1)}, f32[768]{0:T(1024)}, u32[]{:S(2)}) copy-start(f32[768]{0:T(1024)} %copy-done.65) | copy-start | bytes 9220
  411.5 27.3 %copy-start.68 = (f32[768]{0:T(1024)S(1)}, f32[768]{0:T(1024)}, u32[]{:S(2)}) copy-start(f32[768]{0:T(1024)} %copy-done.67) | copy-start | bytes 9220
  411.5 27.3 %copy-start.72 = (f32[256]{0:T(256)S(1)}, f32[256]{0:T(256)}, u32[]{:S(2)}) copy-start(f32[256]{0:T(256)} %copy-done.71) | copy-start | bytes 3076
  411.5 29.0 %copy-start.87 = (f32[256]{0:T(256)S(1)}, f32[256]{0:T(256)}, u32[]{:S(2)}) copy-start(f32[256]{0:T(256)} %copy-done.86) | copy-start | bytes 3076
  411.6 29.0 %copy-start.76 = (f32[256]{0:T(256)S(1)}, f32[256]{0:T(256)}, u32[]{:S(2)}) copy-start(f32[256]{0:T(256)} %copy-done.75) | copy-start | bytes 3076
  411.6 89.4 %copy-start.44 = (bf16[256,768]{1,0:T(8,128)(2,1)S(1)}, bf16[256,768]{1,0:T(8,128)(2,1)}, u32[]{:S(2)}) copy-start(bf16[256,768]{1,0:T(8,128)(2,1)} %param.21) | copy-start | bytes 1179652
  411.6 89.4 %copy-start.77 = (f32[768]{0:T(1024)S(1)}, f32[768]{0:T(1024)}, u32[]{:S(2)}) copy-start(f32[768]{0:T(1024)} %get-tuple-element.502) | copy-start | bytes 9220
  411.6 89.4 %copy-start.78 = (f32[768]{0:T(1024)S(1)}, f32[768]{0:T(1024)}, u32[]{:S(2)}) copy-start(f32[768]{0:T(1024)} %get-tuple-element.659) | copy-start | bytes 9220
  411.6 130.4 %all-gather.17.cloned.1.call-start = ((), (), s32[]{:S(2)}) async-start(), calls=%async_computation.15 | async-start | bytes 1966080 | tf_op jit(solution)/shard_map/all_gather | solution.py:221
  411.7 89.3 %copy-start.24 = (bf16[256,768]{1,0:T(8,128)(2,1)S(1)}, bf16[256,768]{1,0:T(8,128)(2,1)}, u32[]{:S(2)}) copy-start(bf16[256,768]{1,0:T(8,128)(2,1)} %reduce-scatter.11.cloned.1.call-done) | copy-start | bytes 1179652
  438.9 62.1 %copy-start.25 = (bf16[256,768]{1,0:T(8,128)(2,1)S(1)}, bf16[256,768]{1,0:T(8,128)(2,1)}, u32[]{:S(2)}) copy-start(bf16[256,768]{1,0:T(8,128)(2,1)} %reduce-scatter.13.cloned.1.call-done) | copy-start | bytes 1179652
  440.6 101.4 %copy-start.93 = (f32[768]{0:T(1024)S(1)}, f32[768]{0:T(1024)}, u32[]{:S(2)}) copy-start(f32[768]{0:T(1024)} %copy-done.92) | copy-start | bytes 9220
  504.7 177.0 %reduce-scatter.15.cloned.1.call-start = ((), (), s32[]{:S(2)}) async-start(), calls=%async_computation.16 | async-start | bytes 1966080 | tf_op jit(solution)/shard_map/reduce_scatter | solution.py:260
  542.0 7.7 copy-start.100
  552.3 129.5 %reduce-scatter.17.cloned.1.call-start = ((), (), s32[]{:S(2)}) async-start(), calls=%async_computation.17 | async-start | bytes 1966080 | tf_op jit(solution)/shard_map/reduce_scatter | solution.py:257
  557.0 9.2 %copy-start.35 = (bf16[1024,3,64]{0,2,1:T(8,128)(2,1)}, bf16[1024,3,64]{0,2,1:T(8,128)(2,1)S(1)}, u32[]{:S(2)}) copy-start(bf16[1024,3,64]{0,2,1:T(8,128)(2,1)S(1)} %get-tuple-element.1044) | copy-start | bytes 1179652 | tf_op jit(solution)/shard_map/while
  591.9 9.2 %copy-start.35 = (bf16[1024,3,64]{0,2,1:T(8,128)(2,1)}, bf16[1024,3,64]{0,2,1:T(8,128)(2,1)S(1)}, u32[]{:S(2)}) copy-start(bf16[1024,3,64]{0,2,1:T(8,128)(2,1)S(1)} %get-tuple-element.1044) | copy-start | bytes 1179652 | tf_op jit(solution)/shard_map/while
  635.5 230.5 %all-reduce.13.cloned.1.call-start = ((), (), s32[]{:S(2)}) async-start(), calls=%async_computation.18 | async-start | bytes 28311552 | tf_op jit(solution)/shard_map/psum | solution.py:272
  655.8 25.9 %copy-start.12 = (bf16[256,768]{1,0:T(8,128)(2,1)S(1)}, bf16[256,768]{1,0:T(8,128)(2,1)}, u32[]{:S(2)}) copy-start(bf16[256,768]{1,0:T(8,128)(2,1)} %param.20) | copy-start | bytes 1179652
  655.9 25.9 %copy-start.62 = (f32[768]{0:T(1024)S(1)}, f32[768]{0:T(1024)}, u32[]{:S(2)}) copy-start(f32[768]{0:T(1024)} %copy-done.61) | copy-start | bytes 9220
  655.9 25.9 %copy-start.64 = (f32[768]{0:T(1024)S(1)}, f32[768]{0:T(1024)}, u32[]{:S(2)}) copy-start(f32[768]{0:T(1024)} %copy-done.63) | copy-start | bytes 9220
  655.9 25.9 %copy-start.70 = (f32[256]{0:T(256)S(1)}, f32[256]{0:T(256)}, u32[]{:S(2)}) copy-start(f32[256]{0:T(256)} %copy-done.69) | copy-start | bytes 3076
  655.9 27.6 %copy-start.85 = (f32[256]{0:T(256)S(1)}, f32[256]{0:T(256)}, u32[]{:S(2)}) copy-start(f32[256]{0:T(256)} %copy-done.84) | copy-start | bytes 3076
  655.9 27.6 %copy-start.74 = (f32[256]{0:T(256)S(1)}, f32[256]{0:T(256)}, u32[]{:S(2)}) copy-start(f32[256]{0:T(256)} %copy-done.73) | copy-start | bytes 3076
  655.9 69.6 %copy-start.30 = (f32[256,768]{1,0:T(8,128)S(1)}, f32[256,768]{1,0:T(8,128)}, u32[]{:S(2)}) copy-start(f32[256,768]{1,0:T(8,128)} %get-tuple-element.589) | copy-start | bytes 2359300
  725.6 145.7 %copy-start.91 = (f32[2,768]{1,0:T(2,128)}, f32[2,768]{1,0:T(2,128)S(1)}, u32[]{:S(2)}) copy-start(f32[2,768]{1,0:T(2,128)S(1)} %get-tuple-element.1083) | copy-start | bytes 18436
  866.1 6.3 slice-start.6
  (95 other events, 322.0 us)
Sparse Core Ops, SparseCore 0:
  14.0 39.7 all-gather.6
  56.0 36.0 all-gather.8
  107.6 59.1 reduce-scatter.6
  168.2 37.1 all-gather.14
  207.4 35.9 all-gather.10
  245.4 35.9 all-gather.12
  310.3 34.1 reduce-scatter.10
  404.7 34.1 reduce-scatter.12
  441.8 59.2 reduce-scatter.8
  504.9 37.0 all-gather.16
  552.4 34.1 reduce-scatter.14
  635.6 34.1 reduce-scatter.16
  675.0 190.9 all-reduce.12
where the time goes:
time: 897 us; the launch traced here: 885 us
  waiting for transfers between devices  482 us (54%)
  matrix products  165 us (18%)
  local copies, waits for them, and re-layouts  86.4 us (10%)
  blocking collectives  64.5 us (7%)
  other arithmetic  55 us (6%)
  between operations  16 us (2%)
  loops' own time  14.6 us (2%)
    psum x1, waiting for transfers between devices, body(): lax.psum((stacked[0], stacked[1], stacked[2], stacked[3], stacked[4], sta...  138 us
    reduce_scatter x2, waiting for transfers between devices, body(): lax.psum_scatter(branch_term(jnp.int32(0), rows * lax.axis_size('tensor')...  116 us
    all_gather x2, waiting for transfers between devices, body(): lax.all_gather(first_norm.astype(jnp.bfloat16), 'tensor', axis=0, tiled=T...  72.9 us
    all_gather x2, waiting for transfers between devices, body(): grad_all = lax.all_gather(grad_low, 'tensor', axis=0, tiled=True)  71.7 us
    all_gather x2, waiting for transfers between devices, body(): lax.all_gather(second_norm.astype(jnp.bfloat16), 'tensor', axis=0, tiled=...  55 us
    psum x1, blocking collectives, body(): lax.psum((jnp.stack(gain_grads), jnp.stack(shift_grads), jnp.stack(bias_g...  40 us
    dynamic_update_slice x8, local copies, waits for them, and re-layouts, attend_backward(): lax.map(one_block, jnp.arange(count // block, dtype=jnp.int32))  36.9 us
    dot_general x2, matrix products, body(): jnp.dot(mlp_in, w_in[layer_index], preferred_element_type=jnp.float32)  33.8 us
  transfers between devices with their start and end apart: 13, of which 10 were waited for; matrix products, arithmetic and copies ran while one was open for 25% of the time, Pallas kernels for 0%

commit v1 on v0

v1 whole, which is shorter than its diff:
```python
import functools
import math

import jax
import jax.numpy as jnp
from jax import lax
from jax.experimental import pallas as pl
from jax.experimental.pallas import tpu as pltpu
from jax.sharding import PartitionSpec as P

HD = 64
ROT = 16
LEN = 1024
EPS = 1e-05
BF = jnp.bfloat16
F32 = jnp.float32
NEG = -1e30
ROWS = 256
MIB = 1024 * 1024


def dot(a, b, ca, cb):
    return lax.dot_general(a, b, (((ca,), (cb,)), ((), ())), preferred_element_type=F32)


def normalize(rows):
    centre = rows - jnp.mean(rows, axis=-1, keepdims=True)
    scale = lax.rsqrt(jnp.mean(centre * centre, axis=-1, keepdims=True) + EPS)
    return centre * scale, scale


def rope_tables(sign):
    half = ROT // 2
    places = jnp.arange(LEN, dtype=jnp.int32).astype(F32)
    freqs = jnp.exp(jnp.arange(half, dtype=F32) * (-2.0 * math.log(10000.0) / ROT))
    angles = places[:, None] * freqs[None, :]
    cosine, sine = jnp.cos(angles), jnp.sin(angles) * sign
    rest = HD - ROT
    zeros = jnp.zeros_like(sine)
    wide = jnp.zeros((LEN, rest), F32)
    c = jnp.concatenate([cosine, cosine, wide + 1.0], axis=1)
    s_left = jnp.concatenate([-sine, zeros, wide], axis=1)
    s_right = jnp.concatenate([zeros, sine, wide], axis=1)
    return jnp.stack([jnp.concatenate([t, t], axis=1) for t in (c, s_left, s_right)])


def turn(group, tables):
    return (
        group * tables[0]
        + pltpu.roll(group, 128 - ROT // 2, 1) * tables[1]
        + pltpu.roll(group, ROT // 2, 1) * tables[2]
    )


def project_kernel(
    is_raw, x_ref, gain_ref, shift_ref, table_ref, wqkv_ref, bqkv_ref, win_ref, bin_ref,
    attn_ref, mlp_ref, qkv_ref, hidden_ref, slope_ref,
):
    x = x_ref[...].astype(F32)
    n = normalize(x)[0] if is_raw else x
    attn_in = (n * gain_ref[0:1] + shift_ref[0:1]).astype(BF)
    mlp_in = (n * gain_ref[1:2] + shift_ref[1:2]).astype(BF)
    attn_ref[...] = attn_in
    mlp_ref[...] = mlp_in
    projected = dot(attn_in, wqkv_ref[...], 1, 1) + bqkv_ref[...]
    part = projected.shape[1] // 3
    heads = part // HD
    tables = table_ref[...]
    pieces = []
    for g in range(2 * part // 128):
        pieces.append(turn(projected[:, g * 128 : (g + 1) * 128], tables).astype(BF))
    rotated = jnp.concatenate(pieces, axis=1)
    for i in range(2 * heads):
        qkv_ref[i] = rotated[:, i * HD : (i + 1) * HD]
    value = projected[:, 2 * part :].astype(BF)
    for i in range(heads):
        qkv_ref[2 * heads + i] = value[:, i * HD : (i + 1) * HD]
    pre = dot(mlp_in, win_ref[...], 1, 0) + bin_ref[...]
    phi = 0.5 * (1.0 + lax.erf(pre * (1.0 / math.sqrt(2.0))))
    hidden_ref[...] = (pre * phi).astype(BF)
    slope_ref[...] = phi + pre * jnp.exp(-0.5 * pre * pre) * (1.0 / math.sqrt(2.0 * math.pi))


def project(x, is_raw, gains, shifts, tables, wqkv, bqkv, win, bin_):
    count, width = x.shape
    qkv_width, ff = wqkv.shape[0], win.shape[1]
    parts = qkv_width // HD
    whole = lambda *shape: pl.BlockSpec(shape, lambda i: (0,) * len(shape))
    rows = lambda w: pl.BlockSpec((ROWS, w), lambda i: (i, 0))
    per_seq = LEN // ROWS
    return pl.pallas_call(
        functools.partial(project_kernel, is_raw),
        grid=(count // ROWS,),
        in_specs=[
            rows(width), whole(2, width), whole(2, width),
            pl.BlockSpec((3, ROWS, 128), lambda i: (0, i % per_seq, 0)),
            whole(qkv_width, width), whole(1, qkv_width), whole(width, ff), whole(1, ff),
        ],
        out_specs=[
            rows(width), rows(width),
            pl.BlockSpec((parts, ROWS, HD), lambda i: (0, i, 0)),
            rows(ff), rows(ff),
        ],
        out_shape=[
            jax.ShapeDtypeStruct((count, width), BF),
            jax.ShapeDtypeStruct((count, width), BF),
            jax.ShapeDtypeStruct((parts, count, HD), BF),
            jax.ShapeDtypeStruct((count, ff), BF),
            jax.ShapeDtypeStruct((count, ff), F32),
        ],
        compiler_params=pltpu.CompilerParams(vmem_limit_bytes=32 * MIB),
        cost_estimate=pl.CostEstimate(
            flops=2 * count * width * (qkv_width + ff), bytes_accessed=12 * MIB, transcendentals=2 * count * ff
        ),
        name="project",
    )(x, gains, shifts, tables, wqkv, bqkv.reshape(1, -1), win, bin_.reshape(1, -1))


def attend_kernel(qkv_ref, mixed_ref):
    heads = qkv_ref.shape[0] // 3
    row = lax.broadcasted_iota(jnp.int32, (ROWS, ROWS), 0)
    col = lax.broadcasted_iota(jnp.int32, (ROWS, ROWS), 1)
    allowed = col <= row
    for h in range(heads):
        for b in range(LEN // ROWS):
            lo, hi = b * ROWS, (b + 1) * ROWS
            q = (qkv_ref[h, lo:hi].astype(F32) * HD ** (-0.5)).astype(BF)
            s = dot(q, qkv_ref[heads + h, 0:hi], 1, 1)
            edge = jnp.where(allowed, s[:, lo:hi], NEG)
            s = edge if b == 0 else jnp.concatenate([s[:, :lo], edge], axis=1)
            e = jnp.exp(s - jnp.max(s, axis=1, keepdims=True))
            p = (e * (1.0 / jnp.sum(e, axis=1, keepdims=True))).astype(BF)
            o = dot(p, qkv_ref[2 * heads + h, 0:hi], 1, 0)
            mixed_ref[lo:hi, h * HD : (h + 1) * HD] = o.astype(BF)


def attend(qkv):
    parts, count, _ = qkv.shape
    heads = parts // 3
    return pl.pallas_call(
        attend_kernel,
        grid=(count // LEN,),
        in_specs=[pl.BlockSpec((parts, LEN, HD), lambda i: (0, i, 0))],
        out_specs=pl.BlockSpec((LEN, heads * HD), lambda i: (i, 0)),
        out_shape=jax.ShapeDtypeStruct((count, heads * HD), BF),
        compiler_params=pltpu.CompilerParams(vmem_limit_bytes=32 * MIB),
        cost_estimate=pl.CostEstimate(
            flops=8 * count * LEN * HD * heads, bytes_accessed=4 * MIB, transcendentals=count * LEN * heads
        ),
        name="attend",
    )(qkv)


def attend_back_kernel(qkv_ref, grad_ref, wout_ref, table_ref, out_ref, gm_ref, dq_ref, dk_ref, dv_ref):
    heads = qkv_ref.shape[0] // 3
    part = heads * HD
    for b in range(LEN // ROWS):
        lo, hi = b * ROWS, (b + 1) * ROWS
        gm = dot(grad_ref[lo:hi], wout_ref[...], 1, 1).astype(BF)
        for h in range(heads):
            gm_ref[h, lo:hi] = gm[:, h * HD : (h + 1) * HD]
    row = lax.broadcasted_iota(jnp.int32, (ROWS, ROWS), 0)
    col = lax.broadcasted_iota(jnp.int32, (ROWS, ROWS), 1)
    allowed = row <= col
    scale = HD ** (-0.5)
    blocks = LEN // ROWS
    for h in range(heads):
        for b in reversed(range(blocks)):
            lo, hi = b * ROWS, (b + 1) * ROWS
            q = (qkv_ref[h, lo:hi].astype(F32) * scale).astype(BF)
            key = qkv_ref[heads + h, 0:hi]
            s = dot(key, q, 1, 1)
            edge = jnp.where(allowed, s[lo:hi], NEG)
            s = edge if b == 0 else jnp.concatenate([s[:lo], edge], axis=0)
            e = jnp.exp(s - jnp.max(s, axis=0, keepdims=True))
            p = e * (1.0 / jnp.sum(e, axis=0, keepdims=True))
            gm = gm_ref[h, lo:hi]
            dv = dot(p.astype(BF), gm, 1, 0)
            dp = dot(qkv_ref[2 * heads + h, 0:hi], gm, 1, 1)
            delta = jnp.sum(p * dp, axis=0, keepdims=True)
            ds = (p * (dp - delta)).astype(BF)
            dk = dot(ds, q, 1, 0)
            dq = dot(ds, key, 0, 0) * scale
            dq_ref[lo:hi, h * HD : (h + 1) * HD] = dq
            if b == blocks - 1:
                dk_ref[...] = dk
                dv_ref[...] = dv
            else:
                dk_ref[0:hi] += dk
                dv_ref[0:hi] += dv
        dq_ref[:, part + h * HD : part + (h + 1) * HD] = dk_ref[...]
        out_ref[:, 2 * part + h * HD : 2 * part + (h + 1) * HD] = dv_ref[...].astype(BF)
    tables = table_ref[...]
    for g in range(2 * part // 128):
        lanes = slice(g * 128, (g + 1) * 128)
        out_ref[:, lanes] = turn(dq_ref[:, lanes], tables).astype(BF)


def attend_back(qkv, grad_all, wout, tables):
    parts, count, _ = qkv.shape
    heads = parts // 3
    width = grad_all.shape[1]
    part = heads * HD
    return pl.pallas_call(
        attend_back_kernel,
        grid=(count // LEN,),
        in_specs=[
            pl.BlockSpec((parts, LEN, HD), lambda i: (0, i, 0)),
            pl.BlockSpec((LEN, width), lambda i: (i, 0)),
            pl.BlockSpec((part, width), lambda i: (0, 0)),
            pl.BlockSpec((3, LEN, 128), lambda i: (0, 0, 0)),
        ],
        out_specs=pl.BlockSpec((LEN, 3 * part), lambda i: (i, 0)),
        out_shape=jax.ShapeDtypeStruct((count, 3 * part), BF),
        scratch_shapes=[
            pltpu.VMEM((heads, LEN, HD), BF),
            pltpu.VMEM((LEN, 2 * part), F32),
            pltpu.VMEM((LEN, HD), F32),
            pltpu.VMEM((LEN, HD), F32),
        ],
        compiler_params=pltpu.CompilerParams(vmem_limit_bytes=40 * MIB),
        cost_estimate=pl.CostEstimate(
            flops=20 * count * LEN * HD * heads, bytes_accessed=8 * MIB, transcendentals=count * LEN * heads
        ),
        name="attend_back",
    )(qkv, grad_all, wout, tables)


UP = [(0, 1), (1, 2), (2, 3)]
DOWN = [(1, 0), (2, 1), (3, 2)]


def send(x, pairs):
    return lax.ppermute(x, "tensor", pairs)


def gather_rows(x):
    if lax.axis_size("tensor") != 4:
        return lax.all_gather(x, "tensor", axis=0, tiled=True)
    i = lax.axis_index("tensor")
    below, above = send(x, UP), send(x, DOWN)
    a = send(above, [(1, 0), (2, 1)])
    b = send(above, [(2, 0)])
    c = send(below, [(2, 3), (1, 2)])
    d = send(below, [(1, 3)])
    pick = lambda *four: lax.select_n(jnp.broadcast_to(i, x.shape), *four)
    return jnp.concatenate(
        [pick(x, below, c, d), pick(above, x, below, c), pick(a, above, x, below), pick(b, a, above, x)], axis=0
    )


def scatter_sum(x):
    if lax.axis_size("tensor") != 4:
        return lax.psum_scatter(x, "tensor", scatter_dimension=0, tiled=True).astype(F32)
    i = lax.axis_index("tensor")
    rows = x.shape[0] // 4
    own = lambda k: lax.dynamic_slice_in_dim(x, jnp.clip(i + k, 0, 3) * rows, rows, 0)
    a = send(own(2), [(0, 1), (1, 2)])
    b = send(own(3), [(0, 2)])
    c = send(own(-2), [(3, 2), (2, 1)])
    d = send(own(-3), [(3, 1)])
    total = lambda *terms: sum(t.astype(F32) for t in terms)
    from_above = send(total(own(-1), c, d).astype(BF), DOWN)
    from_below = send(total(own(1), a, b).astype(BF), UP)
    return total(own(0), from_above, from_below)


def partner(x, axis, bit):
    return lax.ppermute(x, axis, [(k, k ^ bit) for k in range(lax.axis_size(axis))])


def halve(x, bit):
    side = (lax.axis_index("dp") // bit) % 2
    half = x.shape[0] // 2
    mine = lax.dynamic_slice_in_dim(x, side * half, half, 0)
    other = lax.dynamic_slice_in_dim(x, (1 - side) * half, half, 0)
    return (mine.astype(F32) + partner(other, "dp", bit).astype(F32)).astype(BF)


def unhalve(x, bit):
    side = (lax.axis_index("dp") // bit) % 2
    got = partner(x, "dp", bit)
    return jnp.concatenate([jnp.where(side == 0, x, got), jnp.where(side == 0, got, x)], axis=0)


def sum_dp(x):
    size = lax.axis_size("dp")
    if size % 8 or x.shape[0] % 256:
        return lax.psum(x, "dp")
    y = halve(x, 1)
    half = y.shape[0] // 2
    a, b = halve(halve(y[:half], 2), 4), halve(halve(y[half:], 4), 2)
    if size > 8:
        groups = [[g * 8 + k for g in range(size // 8)] for k in range(8)]
        a, b = lax.psum((a, b), "dp", axis_index_groups=groups)
    a, b = unhalve(unhalve(a, 4), 2), unhalve(unhalve(b, 2), 4)
    return unhalve(jnp.concatenate([a, b], axis=0), 1)


def sum_small(x, axis):
    size = lax.axis_size(axis)
    if size & (size - 1):
        return lax.psum(x, axis)
    bit = 1
    while bit < size:
        x = x + partner(x, axis, bit)
        bit *= 2
    return x


def body(tokens, cotangent, norm_gain, norm_shift, w_qkv, b_qkv, w_out, b_out, w_in, b_in, w_down, b_down):
    layers = w_qkv.shape[0]
    width = tokens.shape[1]
    ff = w_in.shape[2]
    wqkv = w_qkv.transpose(0, 2, 3, 1).reshape(layers, -1, width)
    tables, tables_back = rope_tables(1.0), rope_tables(-1.0)

    stream = tokens.astype(F32)
    gathered = gather_rows(tokens)
    grad_all = gather_rows(cotangent)
    kept = []
    for l in range(layers):
        n_own, scale = normalize(stream)
        if l > 0:
            gathered = gather_rows(n_own.astype(BF))
        attn_in, mlp_in, qkv, hidden, slope = project(
            gathered, l == 0, norm_gain[l], norm_shift[l], tables, wqkv[l], b_qkv[l], w_in[l], b_in[l]
        )
        mixed = attend(qkv)
        branch = (dot(mixed, w_out[l], 1, 0) + dot(hidden, w_down[l], 1, 0)).astype(BF)
        kept.append((n_own, scale, gathered, attn_in, mlp_in, qkv, hidden, slope, mixed))
        stream = stream + scatter_sum(branch) + b_out[l] + b_down[l]

    grad_stream = cotangent.astype(F32)
    big, biases, norms = [None] * layers, [None] * layers, [None] * layers
    for l in reversed(range(layers)):
        n_own, scale, gathered, attn_in, mlp_in, qkv, hidden, slope, mixed = kept[l]
        if l < layers - 1:
            grad_all = gather_rows(grad_stream.astype(BF))
        grad_hidden = dot(grad_all, w_down[l], 1, 1)
        grad_pre = (grad_hidden * slope).astype(BF)
        grad_projected = attend_back(qkv, grad_all, w_out[l], tables_back)
        grad_mlp = dot(grad_pre, w_in[l], 1, 1)
        grad_attn = dot(grad_projected, wqkv[l], 1, 0)
        h = (grad_attn * norm_gain[l, 0] + grad_mlp * norm_gain[l, 1]).astype(BF)
        h_own = scatter_sum(h)
        n_all = normalize(gathered.astype(F32))[0] if l == 0 else gathered.astype(F32)
        norms[l] = jnp.stack(
            [jnp.sum(grad_attn * n_all, 0), jnp.sum(grad_mlp * n_all, 0), jnp.sum(grad_attn, 0), jnp.sum(grad_mlp, 0)]
        )
        biases[l] = (
            jnp.sum(grad_projected.astype(F32), 0), jnp.sum(grad_pre.astype(F32), 0), jnp.sum(grad_all.astype(F32), 0)
        )
        weights = [
            dot(grad_projected, attn_in, 0, 0),
            dot(mixed, grad_all, 0, 0),
            dot(mlp_in, grad_pre, 0, 0),
            dot(hidden, grad_all, 0, 0),
        ]
        packed = jnp.concatenate([w.astype(BF) for w in weights], axis=0)
        big[l] = sum_dp(packed)
        grad_stream = grad_stream + scale * (
            h_own
            - jnp.mean(h_own, axis=-1, keepdims=True)
            - n_own * jnp.mean(h_own * n_own, axis=-1, keepdims=True)
        )

    norm_sums = sum_small(jnp.concatenate(norms, axis=0), "tensor")
    flat = [norm_sums.reshape(-1)] + [v for three in biases for v in three]
    sizes = [v.shape[0] for v in flat]
    small = sum_small(jnp.concatenate(flat).reshape(-1, 128), "dp").reshape(-1)
    pieces = jnp.split(small, [sum(sizes[: k + 1]) for k in range(len(sizes) - 1)])
    norm_sums = pieces[0].reshape(layers, 4, width)
    part = wqkv.shape[1]
    fo = w_out.shape[1]
    grads = jnp.stack(big).astype(F32)
    g_qkv = grads[:, :part].reshape(layers, 3, part // 3, width).transpose(0, 3, 1, 2)
    g_out = grads[:, part : part + fo]
    g_in = grads[:, part + fo : part + fo + width]
    g_down = grads[:, part + fo + width :]
    gb_qkv = jnp.stack([pieces[1 + 3 * l] for l in range(layers)]).reshape(layers, 3, part // 3)
    gb_in = jnp.stack([pieces[2 + 3 * l] for l in range(layers)])
    gb_out = jnp.stack([pieces[3 + 3 * l] for l in range(layers)])
    return (
        stream, grad_stream, norm_sums[:, 0:2], norm_sums[:, 2:4],
        g_qkv, gb_qkv, g_out, gb_out, g_in, gb_in, g_down, gb_out,
    )


def solution(mesh):
    rows = P(("dp", "tensor"), None)
    specs = (
        P(None, None, None, "tensor"), P(None, None, "tensor"), P(None, "tensor", None), P(),
        P(None, None, "tensor"), P(None, "tensor"), P(None, "tensor", None), P(),
    )
    both = (rows, rows, P(), P()) + specs
    return jax.shard_map(body, mesh=mesh, in_specs=both, out_specs=both, check_vma=False)
```

time: 897 us -> 456 us (0.51)
  waiting for transfers between devices: 482 us -> 143 us
  starting transfers between devices: 1.4 us -> 149 us
  matrix products: 165 us -> 29.4 us
  blocking collectives: 64.5 us -> 0 us
  Pallas kernels: 0 us -> 43.3 us
  local copies, waits for them, and re-layouts: 86.4 us -> 45.6 us
  other arithmetic: 55 us -> 38 us
  loops' own time: 14.6 us -> 0 us
  between operations: 16 us -> 2.68 us
    all_gather x6 -> x0, waiting for transfers between devices: 200 us -> none  [the longest x2 72.9 us: body(): lax.all_gather(first_norm.astype(jnp.bfloat16), 'tensor', axis=0, tiled=T...]
    ppermute x0 -> x73, starting transfers between devices: none -> 149 us  [the longest x48 117 us: send(): return lax.ppermute(x, 'tensor', pairs)]
    ppermute x0 -> x73, waiting for transfers between devices: none -> 143 us  [the longest x48 94.6 us: send(): return lax.ppermute(x, 'tensor', pairs)]
    reduce_scatter x6 -> x0, waiting for transfers between devices: 143 us -> none  [the longest x2 116 us: body(): lax.psum_scatter(branch_term(jnp.int32(0), rows * lax.axis_size('tensor')...]
    psum x1 -> x0, waiting for transfers between devices: 138 us -> none  [body(): lax.psum((stacked[0], stacked[1], stacked[2], stacked[3], stacked[4], sta...]
    dot_general x48 -> x18, matrix products: 156 us -> 29.4 us  [dot(): lax.dot_general(a, b, (((ca,), (cb,)), ((), ())), preferred_element_type=...]
    psum x2 -> x0, blocking collectives: 64.5 us -> none  [the longest x1 40 us: body(): lax.psum((jnp.stack(gain_grads), jnp.stack(shift_grads), jnp.stack(bias_g...]
    pallas_call x0 -> x6, Pallas kernels: none -> 43.3 us  [the longest x2 20.8 us: attend_back(): pl.pallas_call(attend_back_kernel, grid=(count // LEN,), in_specs=[pl.Blo...]
  transfers between devices with their start and end apart: 13 -> 73, of which waited for: 10 -> 35; matrix products, arithmetic and copies ran while one was open for 25% -> 16% of each run, Pallas kernels for 0% -> 5%
where the time goes in v1:
time: 456 us; the launch traced here: 451 us
  starting transfers between devices  149 us (33%)
  waiting for transfers between devices  143 us (31%)
  local copies, waits for them, and re-layouts  45.6 us (10%)
  Pallas kernels  43.3 us (9%)
  other arithmetic  38 us (8%)
  matrix products  29.4 us (6%)
    ppermute x48, starting transfers between devices, send(): return lax.ppermute(x, 'tensor', pairs)  117 us
    ppermute x48, waiting for transfers between devices, send(): return lax.ppermute(x, 'tensor', pairs)  94.6 us
    ppermute x25, waiting for transfers between devices, partner(): lax.ppermute(x, axis, [(k, k ^ bit) for k in range(lax.axis_size(axis))])  48.6 us
    ppermute x25, starting transfers between devices, partner(): lax.ppermute(x, axis, [(k, k ^ bit) for k in range(lax.axis_size(axis))])  31.5 us
    dot_general x18, matrix products, dot(): lax.dot_general(a, b, (((ca,), (cb,)), ((), ())), preferred_element_type=...  29.4 us
    pallas_call x2, Pallas kernels, attend_back(): pl.pallas_call(attend_back_kernel, grid=(count // LEN,), in_specs=[pl.Blo...  20.8 us
    unnamed x125, local copies, waits for them, and re-layouts  13 us
    pallas_call x2, Pallas kernels, attend(): pl.pallas_call(attend_kernel, grid=(count // LEN,), in_specs=[pl.BlockSpe...  12.4 us
  transfers between devices with their start and end apart: 73, of which 35 were waited for; matrix products, arithmetic and copies ran while one was open for 16% of the time, Pallas kernels for 5%

profile of v1, /device:TPU:0, one launch (start us, length us, event | category | flops | bytes accessed | tf_op | source)
XLA Modules:
  0.0 450.9 jit_solution(11049006385520099964)
XLA Ops:
  1.9 6.3 %collective-permute-start = (bf16[256,768]{1,0:T(8,128)(2,1)}, bf16[256,768]{1,0:T(8,128)(2,1)}, u32[]{:S(2)}, u32[]{:S(2)}) collective-permute-start(bf16[256,768]{1,0:T(8,128)(2,1)} %param.12), channel_id=1, source_target_pairs={{0,1},{1,2},{2,3},{4,5},{5,6},{6,7},{8,9},{9,10},{10,11},{12,13},{... | collective-permute-start | bytes 1179656 | tf_op jit(solution)/shard_map/ppermute | solution.py:234
  8.3 4.0 collective-permute-start.24
  14.5 3.0 fusion.35
  17.5 2.7 concatenate.83
  27.2 3.0 fusion.10
  36.0 2.8 slice_bitcast_fusion
  38.8 7.9 %collective-permute-done.5 = bf16[256,768]{1,0:T(8,128)(2,1)S(1)} collective-permute-done((bf16[256,768]{1,0:T(8,128)(2,1)}, bf16[256,768]{1,0:T(8,128)(2,1)S(1)}, u32[]{:S(2)}, u32[]{:S(2)}) %collective-permute-start.5) | collective-permute-done | bytes 393248 | tf_op jit(solution)/shard_map/ppermute | solution.py:234
  46.8 6.4 %collective-permute-done.4 = bf16[256,768]{1,0:T(8,128)(2,1)S(1)} collective-permute-done((bf16[256,768]{1,0:T(8,128)(2,1)}, bf16[256,768]{1,0:T(8,128)(2,1)S(1)}, u32[]{:S(2)}, u32[]{:S(2)}) %collective-permute-start.4) | collective-permute-done | bytes 393248 | tf_op jit(solution)/shard_map/ppermute | solution.py:234
  56.1 5.3 %project.2 = (bf16[1024,768]{1,0:T(8,128)(2,1)S(1)}, bf16[1024,768]{1,0:T(8,128)(2,1)S(1)}, bf16[9,1024,64]{2,1,0:T(8,128)(2,1)S(1)}, bf16[1024,768]{1,0:T(8,128)(2,1)S(1)}, f32[1024,768]{1,0:T(8,128)S(1)}) custom-call(bf16[1024,768]{1,0:T(8,128)(2,1)S(1)} %get-tuple-element.83.x_ref, f32[2,768]{1,0:T(2,128)S(1)} %get-tuple-element.181.gain_ref, ...), custom_call_target="tpu_custom_call" | custom-call | flops 2113929216 | bytes 12582912 | tf_op jit(solution)/shard_map/project/pallas_call | solution.py:91
  63.7 6.2 %attend.2 = bf16[1024,192]{1,0:T(8,128)(2,1)S(1)} custom-call(bf16[9,1024,64]{2,1,0:T(8,128)(2,1)S(1)} %get-tuple-element.22.qkv_ref), custom_call_target="tpu_custom_call" | custom-call | flops 1610612736 | bytes 4194304 | tf_op jit(solution)/shard_map/attend/pallas_call | solution.py:140
  75.8 6.4 %collective-permute-start.10 = (bf16[256,768]{1,0:T(8,128)(2,1)}, bf16[256,768]{1,0:T(8,128)(2,1)}, u32[]{:S(2)}, u32[]{:S(2)}) collective-permute-start(bf16[256,768]{1,0:T(8,128)(2,1)} %get-tuple-element.129), channel_id=1, source_target_pairs={{0,2},{4,6},{8,10},{12,14},{16,18},{20,22},{24,26},{28,30}} | collective-permute-start | bytes 1179656 | tf_op jit(solution)/shard_map/ppermute | solution.py:234
  82.1 2.0 collective-permute-start.9
  88.1 3.1 collective-permute-done.10
  91.3 6.4 %collective-permute-done.9 = bf16[256,768]{1,0:T(8,128)(2,1)} collective-permute-done((bf16[256,768]{1,0:T(8,128)(2,1)}, bf16[256,768]{1,0:T(8,128)(2,1)}, u32[]{:S(2)}, u32[]{:S(2)}) %collective-permute-start.9) | collective-permute-done | bytes 393248 | tf_op jit(solution)/shard_map/ppermute | solution.py:234
  97.7 2.7 add_convert_fusion.17
  101.8 5.8 %collective-permute-start.11 = (bf16[256,768]{1,0:T(8,128)(2,1)}, bf16[256,768]{1,0:T(8,128)(2,1)}, u32[]{:S(2)}, u32[]{:S(2)}) collective-permute-start(bf16[256,768]{1,0:T(8,128)(2,1)} %get-tuple-element.127), channel_id=1, source_target_pairs={{0,1},{1,2},{2,3},{4,5},{5,6},{6,7},{8,9},{9,10},{10,11},{12,13},{... | collective-permute-start | bytes 1179656 | tf_op jit(solution)/shard_map/ppermute | solution.py:234
  118.1 6.7 %collective-permute-start.12 = (bf16[256,768]{1,0:T(8,128)(2,1)S(1)}, bf16[256,768]{1,0:T(8,128)(2,1)S(1)}, u32[]{:S(2)}, u32[]{:S(2)}) collective-permute-start(bf16[256,768]{1,0:T(8,128)(2,1)S(1)} %fusion.32), channel_id=1, source_target_pairs={{0,1},{1,2},{2,3},{4,5},{5,6},{6,7},{8,9},{9,10},{10,11},{12,13},{... | collective-permute-start | bytes 1179656 | tf_op jit(solution)/shard_map/ppermute | solution.py:234
  126.8 6.6 %collective-permute-done.15 = bf16[256,768]{1,0:T(8,128)(2,1)S(1)} collective-permute-done((bf16[256,768]{1,0:T(8,128)(2,1)S(1)}, bf16[256,768]{1,0:T(8,128)(2,1)S(1)}, u32[]{:S(2)}, u32[]{:S(2)}) %collective-permute-start.15) | collective-permute-done | bytes 393248 | tf_op jit(solution)/shard_map/ppermute | solution.py:234
  138.0 14.7 %collective-permute-done.28 = bf16[256,768]{1,0:T(8,128)(2,1)S(1)} collective-permute-done((bf16[256,768]{1,0:T(8,128)(2,1)}, bf16[256,768]{1,0:T(8,128)(2,1)S(1)}, u32[]{:S(2)}, u32[]{:S(2)}) %collective-permute-start.28) | collective-permute-done | bytes 393248 | tf_op jit(solution)/shard_map/ppermute | solution.py:234
  152.7 2.7 collective-permute-done.17
  155.4 4.1 collective-permute-done.16
  162.9 4.8 %project.3 = (bf16[1024,768]{1,0:T(8,128)(2,1)S(1)}, bf16[1024,768]{1,0:T(8,128)(2,1)S(1)}, bf16[9,1024,64]{2,1,0:T(8,128)(2,1)S(1)}, bf16[1024,768]{1,0:T(8,128)(2,1)S(1)}, f32[1024,768]{1,0:T(8,128)S(1)}) custom-call(bf16[1024,768]{1,0:T(8,128)(2,1)S(1)} %pad_maximum_fusion.7.x_ref, f32[2,768]{1,0:T(2,128)S(1)} %get-tuple-element.180.gain_ref, ...), custom_call_target="tpu_custom_call" | custom-call | flops 2113929216 | bytes 12582912 | tf_op jit(solution)/shard_map/project/pallas_call | solution.py:91
  171.0 2.6 convert_reduce_fusion.2
  173.6 6.2 %attend.3 = bf16[1024,192]{1,0:T(8,128)(2,1)S(1)} custom-call(bf16[9,1024,64]{2,1,0:T(8,128)(2,1)S(1)} %get-tuple-element.24.qkv_ref), custom_call_target="tpu_custom_call" | custom-call | flops 1610612736 | bytes 4194304 | tf_op jit(solution)/shard_map/attend/pallas_call | solution.py:140
  179.8 10.5 %attend_back.2 = bf16[1024,576]{1,0:T(8,128)(2,1)S(1)} custom-call(bf16[9,1024,64]{2,1,0:T(8,128)(2,1)S(1)} %get-tuple-element.24.qkv_ref, bf16[1024,768]{1,0:T(8,128)(2,1)S(1)} %get-tuple-element.79.grad_ref, bf16[192,768]{1,0:T(8,128)(2,1)S(1)} %get-tuple-element.158.wout_ref, f32[3,1024,128]{2,1,0:T(8,128)S(1)} %get-tuple-element.159.table_ref), custom_call_target="tpu_custom_call" | custom-call | flops 4026531840 | bytes 8388608 | tf_op jit(solution)/shard_map/attend_back/pallas_call | solution.py:204
  193.4 2.6 fusion.40
  196.9 9.2 %collective-permute-start.34 = (bf16[256,768]{1,0:T(8,128)(2,1)S(1)}, bf16[256,768]{1,0:T(8,128)(2,1)S(1)}, u32[]{:S(2)}, u32[]{:S(2)}) collective-permute-start(bf16[256,768]{1,0:T(8,128)(2,1)S(1)} %get-tuple-element.117), channel_id=1, source_target_pairs={{0,2},{4,6},{8,10},{12,14},{16,18},{20,22},{24,26},{28,30}} | collective-permute-start | bytes 1179656 | tf_op jit(solution)/shard_map/ppermute | solution.py:234
  210.6 7.4 %collective-permute-start.22 = (bf16[256,768]{1,0:T(8,128)(2,1)S(1)}, bf16[256,768]{1,0:T(8,128)(2,1)S(1)}, u32[]{:S(2)}, u32[]{:S(2)}) collective-permute-start(bf16[256,768]{1,0:T(8,128)(2,1)S(1)} %get-tuple-element.123), channel_id=1, source_target_pairs={{0,2},{4,6},{8,10},{12,14},{16,18},{20,22},{24,26},{28,30}} | collective-permute-start | bytes 1179656 | tf_op jit(solution)/shard_map/ppermute | solution.py:234
  219.4 4.6 %collective-permute-done.33 = bf16[256,768]{1,0:T(8,128)(2,1)S(1)} collective-permute-done((bf16[256,768]{1,0:T(8,128)(2,1)S(1)}, bf16[256,768]{1,0:T(8,128)(2,1)S(1)}, u32[]{:S(2)}, u32[]{:S(2)}) %collective-permute-start.33) | collective-permute-done | bytes 393248 | tf_op jit(solution)/shard_map/ppermute | solution.py:234
  226.4 5.6 %collective-permute-start.35 = (bf16[256,768]{1,0:T(8,128)(2,1)S(1)}, bf16[256,768]{1,0:T(8,128)(2,1)S(1)}, u32[]{:S(2)}, u32[]{:S(2)}) collective-permute-start(bf16[256,768]{1,0:T(8,128)(2,1)S(1)} %get-tuple-element.115), channel_id=1, source_target_pairs={{0,1},{1,2},{2,3},{4,5},{5,6},{6,7},{8,9},{9,10},{10,11},{12,13},{... | collective-permute-start | bytes 1179656 | tf_op jit(solution)/shard_map/ppermute | solution.py:234
  232.6 8.4 %collective-permute-done.21 = bf16[256,768]{1,0:T(8,128)(2,1)S(1)} collective-permute-done((bf16[256,768]{1,0:T(8,128)(2,1)S(1)}, bf16[256,768]{1,0:T(8,128)(2,1)S(1)}, u32[]{:S(2)}, u32[]{:S(2)}) %collective-permute-start.21) | collective-permute-done | bytes 393248 | tf_op jit(solution)/shard_map/ppermute | solution.py:234
  242.5 5.0 %collective-permute-start.23 = (bf16[256,768]{1,0:T(8,128)(2,1)S(1)}, bf16[256,768]{1,0:T(8,128)(2,1)S(1)}, u32[]{:S(2)}, u32[]{:S(2)}) collective-permute-start(bf16[256,768]{1,0:T(8,128)(2,1)S(1)} %get-tuple-element.121), channel_id=1, source_target_pairs={{0,1},{1,2},{2,3},{4,5},{5,6},{6,7},{8,9},{9,10},{10,11},{12,13},{... | collective-permute-start | bytes 1179656 | tf_op jit(solution)/shard_map/ppermute | solution.py:234
  251.7 4.0 collective-permute-done.23
  258.6 5.0 %collective-permute-start.36 = (bf16[256,768]{1,0:T(8,128)(2,1)S(1)}, bf16[256,768]{1,0:T(8,128)(2,1)S(1)}, u32[]{:S(2)}, u32[]{:S(2)}) collective-permute-start(bf16[256,768]{1,0:T(8,128)(2,1)S(1)} %get-tuple-element.84), channel_id=1, source_target_pairs={{0,1},{1,2},{2,3},{4,5},{5,6},{6,7},{8,9},{9,10},{10,11},{12,13},{... | collective-permute-start | bytes 1179656 | tf_op jit(solution)/shard_map/ppermute | solution.py:234
  264.1 4.9 %collective-permute-done.39 = bf16[256,768]{1,0:T(8,128)(2,1)S(1)} collective-permute-done((bf16[256,768]{1,0:T(8,128)(2,1)S(1)}, bf16[256,768]{1,0:T(8,128)(2,1)S(1)}, u32[]{:S(2)}, u32[]{:S(2)}) %collective-permute-start.39) | collective-permute-done | bytes 393248 | tf_op jit(solution)/shard_map/ppermute | solution.py:234
  275.0 8.9 %collective-permute-done.41 = bf16[256,768]{1,0:T(8,128)(2,1)S(1)} collective-permute-done((bf16[256,768]{1,0:T(8,128)(2,1)S(1)}, bf16[256,768]{1,0:T(8,128)(2,1)S(1)}, u32[]{:S(2)}, u32[]{:S(2)}) %collective-permute-start.41) | collective-permute-done | bytes 393248 | tf_op jit(solution)/shard_map/ppermute | solution.py:234
  283.9 4.8 %collective-permute-done.40 = bf16[256,768]{1,0:T(8,128)(2,1)S(1)} collective-permute-done((bf16[256,768]{1,0:T(8,128)(2,1)S(1)}, bf16[256,768]{1,0:T(8,128)(2,1)S(1)}, u32[]{:S(2)}, u32[]{:S(2)}) %collective-permute-start.40) | collective-permute-done | bytes 393248 | tf_op jit(solution)/shard_map/ppermute | solution.py:234
  290.3 2.5 convolution_convert_fusion.2
  292.7 10.4 %attend_back.3 = bf16[1024,576]{1,0:T(8,128)(2,1)S(1)} custom-call(bf16[9,1024,64]{2,1,0:T(8,128)(2,1)S(1)} %copy-done.14, bf16[1024,768]{1,0:T(8,128)(2,1)S(1)} %get-tuple-element.81.grad_ref, bf16[192,768]{1,0:T(8,128)(2,1)S(1)} %get-tuple-element.157.wout_ref, f32[3,1024,128]{2,1,0:T(8,128)S(1)} %copy-done.1), custom_call_target="tpu_custom_call" | custom-call | flops 4026531840 | bytes 8388608 | tf_op jit(solution)/shard_map/attend_back/pallas_call | solution.py:204
  306.2 2.1 convolution_convert_fusion.5
  308.3 2.5 convolution_convert_fusion.3
  310.7 3.1 fusion.42
  313.9 2.5 collective-permute-start.48
  318.2 3.9 collective-permute-start.49
  326.7 6.2 %collective-permute-start.46 = (bf16[256,768]{1,0:T(8,128)(2,1)}, bf16[256,768]{1,0:T(8,128)(2,1)}, u32[]{:S(2)}, u32[]{:S(2)}) collective-permute-start(bf16[256,768]{1,0:T(8,128)(2,1)} %get-tuple-element.111), channel_id=1, source_target_pairs={{0,2},{4,6},{8,10},{12,14},{16,18},{20,22},{24,26},{28,30}} | collective-permute-start | bytes 1179656 | tf_op jit(solution)/shard_map/ppermute | solution.py:234
  334.9 2.1 collective-permute-done.51
  350.7 7.0 %collective-permute-done.68 = bf16[288,768]{1,0:T(8,128)(2,1)S(1)} collective-permute-done((bf16[288,768]{1,0:T(8,128)(2,1)S(1)}, bf16[288,768]{1,0:T(8,128)(2,1)S(1)}, u32[]{:S(2)}, u32[]{:S(2)}) %collective-permute-start.68) | collective-permute-done | bytes 442400 | tf_op jit(solution)/shard_map/ppermute | solution.py:269
  359.5 2.6 collective-permute-start.65
  367.4 2.5 collective-permute-done.70
  375.9 9.0 %collective-permute-start.47 = (bf16[256,768]{1,0:T(8,128)(2,1)S(1)}, bf16[256,768]{1,0:T(8,128)(2,1)S(1)}, u32[]{:S(2)}, u32[]{:S(2)}) collective-permute-start(bf16[256,768]{1,0:T(8,128)(2,1)S(1)} %get-tuple-element.109), channel_id=1, source_target_pairs={{0,1},{1,2},{2,3},{4,5},{5,6},{6,7},{8,9},{9,10},{10,11},{12,13},{... | collective-permute-start | bytes 1179656 | tf_op jit(solution)/shard_map/ppermute | solution.py:234
  384.9 2.1 collective-permute-start.67
  387.2 2.0 add_convert_fusion.1
  390.4 6.4 %collective-permute-done.67 = bf16[288,768]{1,0:T(8,128)(2,1)S(1)} collective-permute-done((bf16[288,768]{1,0:T(8,128)(2,1)S(1)}, bf16[288,768]{1,0:T(8,128)(2,1)S(1)}, u32[]{:S(2)}, u32[]{:S(2)}) %collective-permute-start.67) | collective-permute-done | bytes 442400 | tf_op jit(solution)/shard_map/ppermute | solution.py:269
  397.0 2.5 collective-permute-start.54
  400.0 8.2 %collective-permute-done.54 = bf16[288,768]{1,0:T(8,128)(2,1)S(1)} collective-permute-done((bf16[288,768]{1,0:T(8,128)(2,1)S(1)}, bf16[288,768]{1,0:T(8,128)(2,1)S(1)}, u32[]{:S(2)}, u32[]{:S(2)}) %collective-permute-start.54) | collective-permute-done | bytes 442400 | tf_op jit(solution)/shard_map/ppermute | solution.py:269
  408.4 3.2 collective-permute-done.59
  411.7 2.5 collective-permute-start.60
  416.1 3.1 collective-permute-done.60
  419.4 3.7 collective-permute-done.56
  425.5 2.3 collective-permute-done.61
  428.0 3.5 collective-permute-done.57
  439.7 4.0 maximum_convert_fusion
  443.7 2.0 slice.157
  445.8 4.3 fusion.47
  (365 shorter events, 138.6 us)
Async XLA Ops:
  0.6 31.1 %collective-permute-start.3 = (bf16[256,768]{1,0:T(8,128)(2,1)}, bf16[256,768]{1,0:T(8,128)(2,1)}, u32[]{:S(2)}, u32[]{:S(2)}) collective-permute-start(bf16[256,768]{1,0:T(8,128)(2,1)} %param.12), channel_id=1, source_target_pairs={{1,0},{2,1},{3,2},{5,4},{6,5},{7,6},{9,8},{10,9},{11,10},{13,12},{... | collective-permute-start | bytes 1179656 | tf_op jit(solution)/shard_map/ppermute | solution.py:234
  1.9 32.4 %collective-permute-start = (bf16[256,768]{1,0:T(8,128)(2,1)}, bf16[256,768]{1,0:T(8,128)(2,1)}, u32[]{:S(2)}, u32[]{:S(2)}) collective-permute-start(bf16[256,768]{1,0:T(8,128)(2,1)} %param.12), channel_id=1, source_target_pairs={{0,1},{1,2},{2,3},{4,5},{5,6},{6,7},{8,9},{9,10},{10,11},{12,13},{... | collective-permute-start | bytes 1179656 | tf_op jit(solution)/shard_map/ppermute | solution.py:234
  8.3 100.7 %collective-permute-start.24 = (bf16[256,768]{1,0:T(8,128)(2,1)}, bf16[256,768]{1,0:T(8,128)(2,1)}, u32[]{:S(2)}, u32[]{:S(2)}) collective-permute-start(bf16[256,768]{1,0:T(8,128)(2,1)} %param.13), channel_id=1, source_target_pairs={{0,1},{1,2},{2,3},{4,5},{5,6},{6,7},{8,9},{9,10},{10,11},{12,13},{... | collective-permute-start | bytes 1179656 | tf_op jit(solution)/shard_map/ppermute | solution.py:234
  31.7 15.1 %collective-permute-start.5 = (bf16[256,768]{1,0:T(8,128)(2,1)}, bf16[256,768]{1,0:T(8,128)(2,1)S(1)}, u32[]{:S(2)}, u32[]{:S(2)}) collective-permute-start(bf16[256,768]{1,0:T(8,128)(2,1)} %collective-permute-done.3), channel_id=1, source_target_pairs={{2,0},{6,4},{10,8},{14,12},{18,16},{22,20},{26,24},{30,28}} | collective-permute-start | bytes 1179656 | tf_op jit(solution)/shard_map/ppermute | solution.py:234
  33.0 20.1 %collective-permute-start.4 = (bf16[256,768]{1,0:T(8,128)(2,1)}, bf16[256,768]{1,0:T(8,128)(2,1)S(1)}, u32[]{:S(2)}, u32[]{:S(2)}) collective-permute-start(bf16[256,768]{1,0:T(8,128)(2,1)} %collective-permute-done.3), channel_id=1, source_target_pairs={{1,0},{2,1},{5,4},{6,5},{9,8},{10,9},{13,12},{14,13},{17,16},{18,1... | collective-permute-start | bytes 1179656 | tf_op jit(solution)/shard_map/ppermute | solution.py:234
  34.3 18.8 %collective-permute-start.2 = (bf16[256,768]{1,0:T(8,128)(2,1)}, bf16[256,768]{1,0:T(8,128)(2,1)S(1)}, u32[]{:S(2)}, u32[]{:S(2)}) collective-permute-start(bf16[256,768]{1,0:T(8,128)(2,1)} %collective-permute-done), channel_id=1, source_target_pairs={{1,3},{5,7},{9,11},{13,15},{17,19},{21,23},{25,27},{29,31}} | collective-permute-start | bytes 1179656 | tf_op jit(solution)/shard_map/ppermute | solution.py:234
  35.0 18.1 %collective-permute-start.1 = (bf16[256,768]{1,0:T(8,128)(2,1)}, bf16[256,768]{1,0:T(8,128)(2,1)S(1)}, u32[]{:S(2)}, u32[]{:S(2)}) collective-permute-start(bf16[256,768]{1,0:T(8,128)(2,1)} %collective-permute-done), channel_id=1, source_target_pairs={{2,3},{1,2},{6,7},{5,6},{10,11},{9,10},{14,15},{13,14},{18,19},{17... | collective-permute-start | bytes 1179656 | tf_op jit(solution)/shard_map/ppermute | solution.py:234
  74.3 12.5 %collective-permute-start.6 = (bf16[256,768]{1,0:T(8,128)(2,1)}, bf16[256,768]{1,0:T(8,128)(2,1)}, u32[]{:S(2)}, u32[]{:S(2)}) collective-permute-start(bf16[256,768]{1,0:T(8,128)(2,1)} %get-tuple-element.128), channel_id=1, source_target_pairs={{3,2},{2,1},{7,6},{6,5},{11,10},{10,9},{15,14},{14,13},{19,18},{18... | collective-permute-start | bytes 1179656 | tf_op jit(solution)/shard_map/ppermute | solution.py:234
  75.8 15.5 %collective-permute-start.10 = (bf16[256,768]{1,0:T(8,128)(2,1)}, bf16[256,768]{1,0:T(8,128)(2,1)}, u32[]{:S(2)}, u32[]{:S(2)}) collective-permute-start(bf16[256,768]{1,0:T(8,128)(2,1)} %get-tuple-element.129), channel_id=1, source_target_pairs={{0,2},{4,6},{8,10},{12,14},{16,18},{20,22},{24,26},{28,30}} | collective-permute-start | bytes 1179656 | tf_op jit(solution)/shard_map/ppermute | solution.py:234
  82.1 15.6 %collective-permute-start.9 = (bf16[256,768]{1,0:T(8,128)(2,1)}, bf16[256,768]{1,0:T(8,128)(2,1)}, u32[]{:S(2)}, u32[]{:S(2)}) collective-permute-start(bf16[256,768]{1,0:T(8,128)(2,1)} %get-tuple-element.130), channel_id=1, source_target_pairs={{0,1},{1,2},{4,5},{5,6},{8,9},{9,10},{12,13},{13,14},{16,17},{17,1... | collective-permute-start | bytes 1179656 | tf_op jit(solution)/shard_map/ppermute | solution.py:234
  84.2 13.5 %collective-permute-start.7 = (bf16[256,768]{1,0:T(8,128)(2,1)}, bf16[256,768]{1,0:T(8,128)(2,1)}, u32[]{:S(2)}, u32[]{:S(2)}) collective-permute-start(bf16[256,768]{1,0:T(8,128)(2,1)} %get-tuple-element.131), channel_id=1, source_target_pairs={{3,1},{7,5},{11,9},{15,13},{19,17},{23,21},{27,25},{31,29}} | collective-permute-start | bytes 1179656 | tf_op jit(solution)/shard_map/ppermute | solution.py:234
  86.8 23.5 %collective-permute-start.27 = (bf16[256,768]{1,0:T(8,128)(2,1)}, bf16[256,768]{1,0:T(8,128)(2,1)}, u32[]{:S(2)}, u32[]{:S(2)}) collective-permute-start(bf16[256,768]{1,0:T(8,128)(2,1)} %param.13), channel_id=1, source_target_pairs={{1,0},{2,1},{3,2},{5,4},{6,5},{7,6},{9,8},{10,9},{11,10},{13,12},{... | collective-permute-start | bytes 1179656 | tf_op jit(solution)/shard_map/ppermute | solution.py:234
  100.5 12.9 %collective-permute-start.8 = (bf16[256,768]{1,0:T(8,128)(2,1)}, bf16[256,768]{1,0:T(8,128)(2,1)}, u32[]{:S(2)}, u32[]{:S(2)}) collective-permute-start(bf16[256,768]{1,0:T(8,128)(2,1)} %get-tuple-element.126), channel_id=1, source_target_pairs={{1,0},{2,1},{3,2},{5,4},{6,5},{7,6},{9,8},{10,9},{11,10},{13,12},{... | collective-permute-start | bytes 1179656 | tf_op jit(solution)/shard_map/ppermute | solution.py:234
  101.8 12.8 %collective-permute-start.11 = (bf16[256,768]{1,0:T(8,128)(2,1)}, bf16[256,768]{1,0:T(8,128)(2,1)}, u32[]{:S(2)}, u32[]{:S(2)}) collective-permute-start(bf16[256,768]{1,0:T(8,128)(2,1)} %get-tuple-element.127), channel_id=1, source_target_pairs={{0,1},{1,2},{2,3},{4,5},{5,6},{6,7},{8,9},{9,10},{10,11},{12,13},{... | collective-permute-start | bytes 1179656 | tf_op jit(solution)/shard_map/ppermute | solution.py:234
  109.0 16.5 %collective-permute-start.26 = (bf16[256,768]{1,0:T(8,128)(2,1)}, bf16[256,768]{1,0:T(8,128)(2,1)S(1)}, u32[]{:S(2)}, u32[]{:S(2)}) collective-permute-start(bf16[256,768]{1,0:T(8,128)(2,1)} %collective-permute-done.24), channel_id=1, source_target_pairs={{1,3},{5,7},{9,11},{13,15},{17,19},{21,23},{25,27},{29,31}} | collective-permute-start | bytes 1179656 | tf_op jit(solution)/shard_map/ppermute | solution.py:234
  109.7 25.0 %collective-permute-start.25 = (bf16[256,768]{1,0:T(8,128)(2,1)}, bf16[256,768]{1,0:T(8,128)(2,1)S(1)}, u32[]{:S(2)}, u32[]{:S(2)}) collective-permute-start(bf16[256,768]{1,0:T(8,128)(2,1)} %collective-permute-done.24), channel_id=1, source_target_pairs={{2,3},{1,2},{6,7},{5,6},{10,11},{9,10},{14,15},{13,14},{18,19},{17... | collective-permute-start | bytes 1179656 | tf_op jit(solution)/shard_map/ppermute | solution.py:234
  110.4 26.3 %collective-permute-start.29 = (bf16[256,768]{1,0:T(8,128)(2,1)}, bf16[256,768]{1,0:T(8,128)(2,1)S(1)}, u32[]{:S(2)}, u32[]{:S(2)}) collective-permute-start(bf16[256,768]{1,0:T(8,128)(2,1)} %collective-permute-done.27), channel_id=1, source_target_pairs={{2,0},{6,4},{10,8},{14,12},{18,16},{22,20},{26,24},{30,28}} | collective-permute-start | bytes 1179656 | tf_op jit(solution)/shard_map/ppermute | solution.py:234
  116.8 16.6 %collective-permute-start.15 = (bf16[256,768]{1,0:T(8,128)(2,1)S(1)}, bf16[256,768]{1,0:T(8,128)(2,1)S(1)}, u32[]{:S(2)}, u32[]{:S(2)}) collective-permute-start(bf16[256,768]{1,0:T(8,128)(2,1)S(1)} %fusion.32), channel_id=1, source_target_pairs={{1,0},{2,1},{3,2},{5,4},{6,5},{7,6},{9,8},{10,9},{11,10},{13,12},{... | collective-permute-start | bytes 1179656 | tf_op jit(solution)/shard_map/ppermute | solution.py:234
  118.1 17.9 %collective-permute-start.12 = (bf16[256,768]{1,0:T(8,128)(2,1)S(1)}, bf16[256,768]{1,0:T(8,128)(2,1)S(1)}, u32[]{:S(2)}, u32[]{:S(2)}) collective-permute-start(bf16[256,768]{1,0:T(8,128)(2,1)S(1)} %fusion.32), channel_id=1, source_target_pairs={{0,1},{1,2},{2,3},{4,5},{5,6},{6,7},{8,9},{9,10},{10,11},{12,13},{... | collective-permute-start | bytes 1179656 | tf_op jit(solution)/shard_map/ppermute | solution.py:234
  125.5 27.3 %collective-permute-start.28 = (bf16[256,768]{1,0:T(8,128)(2,1)}, bf16[256,768]{1,0:T(8,128)(2,1)S(1)}, u32[]{:S(2)}, u32[]{:S(2)}) collective-permute-start(bf16[256,768]{1,0:T(8,128)(2,1)} %collective-permute-done.27), channel_id=1, source_target_pairs={{1,0},{2,1},{5,4},{6,5},{9,8},{10,9},{13,12},{14,13},{17,16},{18,1... | collective-permute-start | bytes 1179656 | tf_op jit(solution)/shard_map/ppermute | solution.py:234
  133.4 22.0 %collective-permute-start.17 = (bf16[256,768]{1,0:T(8,128)(2,1)S(1)}, bf16[256,768]{1,0:T(8,128)(2,1)S(1)}, u32[]{:S(2)}, u32[]{:S(2)}) collective-permute-start(bf16[256,768]{1,0:T(8,128)(2,1)S(1)} %collective-permute-done.15), channel_id=1, source_target_pairs={{2,0},{6,4},{10,8},{14,12},{18,16},{22,20},{26,24},{30,28}} | collective-permute-start | bytes 1179656 | tf_op jit(solution)/shard_map/ppermute | solution.py:234
  134.7 24.8 %collective-permute-start.16 = (bf16[256,768]{1,0:T(8,128)(2,1)S(1)}, bf16[256,768]{1,0:T(8,128)(2,1)S(1)}, u32[]{:S(2)}, u32[]{:S(2)}) collective-permute-start(bf16[256,768]{1,0:T(8,128)(2,1)S(1)} %collective-permute-done.15), channel_id=1, source_target_pairs={{1,0},{2,1},{5,4},{6,5},{9,8},{10,9},{13,12},{14,13},{17,16},{18,1... | collective-permute-start | bytes 1179656 | tf_op jit(solution)/shard_map/ppermute | solution.py:234
  136.0 23.5 %collective-permute-start.14 = (bf16[256,768]{1,0:T(8,128)(2,1)S(1)}, bf16[256,768]{1,0:T(8,128)(2,1)S(1)}, u32[]{:S(2)}, u32[]{:S(2)}) collective-permute-start(bf16[256,768]{1,0:T(8,128)(2,1)S(1)} %collective-permute-done.12), channel_id=1, source_target_pairs={{1,3},{5,7},{9,11},{13,15},{17,19},{21,23},{25,27},{29,31}} | collective-permute-start | bytes 1179656 | tf_op jit(solution)/shard_map/ppermute | solution.py:234
  136.7 22.8 %collective-permute-start.13 = (bf16[256,768]{1,0:T(8,128)(2,1)S(1)}, bf16[256,768]{1,0:T(8,128)(2,1)S(1)}, u32[]{:S(2)}, u32[]{:S(2)}) collective-permute-start(bf16[256,768]{1,0:T(8,128)(2,1)S(1)} %collective-permute-done.12), channel_id=1, source_target_pairs={{2,3},{1,2},{6,7},{5,6},{10,11},{9,10},{14,15},{13,14},{18,19},{17... | collective-permute-start | bytes 1179656 | tf_op jit(solution)/shard_map/ppermute | solution.py:234
  196.1 14.5 %collective-permute-start.30 = (bf16[256,768]{1,0:T(8,128)(2,1)S(1)}, bf16[256,768]{1,0:T(8,128)(2,1)S(1)}, u32[]{:S(2)}, u32[]{:S(2)}) collective-permute-start(bf16[256,768]{1,0:T(8,128)(2,1)S(1)} %get-tuple-element.116), channel_id=1, source_target_pairs={{3,2},{2,1},{7,6},{6,5},{11,10},{10,9},{15,14},{14,13},{19,18},{18... | collective-permute-start | bytes 1179656 | tf_op jit(solution)/shard_map/ppermute | solution.py:234
  196.9 21.2 %collective-permute-start.34 = (bf16[256,768]{1,0:T(8,128)(2,1)S(1)}, bf16[256,768]{1,0:T(8,128)(2,1)S(1)}, u32[]{:S(2)}, u32[]{:S(2)}) collective-permute-start(bf16[256,768]{1,0:T(8,128)(2,1)S(1)} %get-tuple-element.117), channel_id=1, source_target_pairs={{0,2},{4,6},{8,10},{12,14},{16,18},{20,22},{24,26},{28,30}} | collective-permute-start | bytes 1179656 | tf_op jit(solution)/shard_map/ppermute | solution.py:234
  206.1 18.0 %collective-permute-start.33 = (bf16[256,768]{1,0:T(8,128)(2,1)S(1)}, bf16[256,768]{1,0:T(8,128)(2,1)S(1)}, u32[]{:S(2)}, u32[]{:S(2)}) collective-permute-start(bf16[256,768]{1,0:T(8,128)(2,1)S(1)} %get-tuple-element.118), channel_id=1, source_target_pairs={{0,1},{1,2},{4,5},{5,6},{8,9},{9,10},{12,13},{13,14},{16,17},{17,1... | collective-permute-start | bytes 1179656 | tf_op jit(solution)/shard_map/ppermute | solution.py:234
  207.4 17.3 %collective-permute-start.31 = (bf16[256,768]{1,0:T(8,128)(2,1)S(1)}, bf16[256,768]{1,0:T(8,128)(2,1)S(1)}, u32[]{:S(2)}, u32[]{:S(2)}) collective-permute-start(bf16[256,768]{1,0:T(8,128)(2,1)S(1)} %get-tuple-element.119), channel_id=1, source_target_pairs={{3,1},{7,5},{11,9},{15,13},{19,17},{23,21},{27,25},{31,29}} | collective-permute-start | bytes 1179656 | tf_op jit(solution)/shard_map/ppermute | solution.py:234
  208.8 17.6 %collective-permute-start.18 = (bf16[256,768]{1,0:T(8,128)(2,1)S(1)}, bf16[256,768]{1,0:T(8,128)(2,1)S(1)}, u32[]{:S(2)}, u32[]{:S(2)}) collective-permute-start(bf16[256,768]{1,0:T(8,128)(2,1)S(1)} %get-tuple-element.122), channel_id=1, source_target_pairs={{3,2},{2,1},{7,6},{6,5},{11,10},{10,9},{15,14},{14,13},{19,18},{18... | collective-permute-start | bytes 1179656 | tf_op jit(solution)/shard_map/ppermute | solution.py:234
  210.6 21.9 %collective-permute-start.22 = (bf16[256,768]{1,0:T(8,128)(2,1)S(1)}, bf16[256,768]{1,0:T(8,128)(2,1)S(1)}, u32[]{:S(2)}, u32[]{:S(2)}) collective-permute-start(bf16[256,768]{1,0:T(8,128)(2,1)S(1)} %get-tuple-element.123), channel_id=1, source_target_pairs={{0,2},{4,6},{8,10},{12,14},{16,18},{20,22},{24,26},{28,30}} | collective-permute-start | bytes 1179656 | tf_op jit(solution)/shard_map/ppermute | solution.py:234
  218.1 22.9 %collective-permute-start.21 = (bf16[256,768]{1,0:T(8,128)(2,1)S(1)}, bf16[256,768]{1,0:T(8,128)(2,1)S(1)}, u32[]{:S(2)}, u32[]{:S(2)}) collective-permute-start(bf16[256,768]{1,0:T(8,128)(2,1)S(1)} %get-tuple-element.124), channel_id=1, source_target_pairs={{0,1},{1,2},{4,5},{5,6},{8,9},{9,10},{12,13},{13,14},{16,17},{17,1... | collective-permute-start | bytes 1179656 | tf_op jit(solution)/shard_map/ppermute | solution.py:234
  224.1 16.9 %collective-permute-start.19 = (bf16[256,768]{1,0:T(8,128)(2,1)S(1)}, bf16[256,768]{1,0:T(8,128)(2,1)S(1)}, u32[]{:S(2)}, u32[]{:S(2)}) collective-permute-start(bf16[256,768]{1,0:T(8,128)(2,1)S(1)} %get-tuple-element.125), channel_id=1, source_target_pairs={{3,1},{7,5},{11,9},{15,13},{19,17},{23,21},{27,25},{31,29}} | collective-permute-start | bytes 1179656 | tf_op jit(solution)/shard_map/ppermute | solution.py:234
  225.0 22.5 %collective-permute-start.32 = (bf16[256,768]{1,0:T(8,128)(2,1)S(1)}, bf16[256,768]{1,0:T(8,128)(2,1)S(1)}, u32[]{:S(2)}, u32[]{:S(2)}) collective-permute-start(bf16[256,768]{1,0:T(8,128)(2,1)S(1)} %get-tuple-element.114), channel_id=1, source_target_pairs={{1,0},{2,1},{3,2},{5,4},{6,5},{7,6},{9,8},{10,9},{11,10},{13,12},{... | collective-permute-start | bytes 1179656 | tf_op jit(solution)/shard_map/ppermute | solution.py:234
  226.4 23.0 %collective-permute-start.35 = (bf16[256,768]{1,0:T(8,128)(2,1)S(1)}, bf16[256,768]{1,0:T(8,128)(2,1)S(1)}, u32[]{:S(2)}, u32[]{:S(2)}) collective-permute-start(bf16[256,768]{1,0:T(8,128)(2,1)S(1)} %get-tuple-element.115), channel_id=1, source_target_pairs={{0,1},{1,2},{2,3},{4,5},{5,6},{6,7},{8,9},{9,10},{10,11},{12,13},{... | collective-permute-start | bytes 1179656 | tf_op jit(solution)/shard_map/ppermute | solution.py:234
  241.2 10.5 %collective-permute-start.20 = (bf16[256,768]{1,0:T(8,128)(2,1)S(1)}, bf16[256,768]{1,0:T(8,128)(2,1)S(1)}, u32[]{:S(2)}, u32[]{:S(2)}) collective-permute-start(bf16[256,768]{1,0:T(8,128)(2,1)S(1)} %get-tuple-element.120), channel_id=1, source_target_pairs={{1,0},{2,1},{3,2},{5,4},{6,5},{7,6},{9,8},{10,9},{11,10},{13,12},{... | collective-permute-start | bytes 1179656 | tf_op jit(solution)/shard_map/ppermute | solution.py:234
  242.5 13.2 %collective-permute-start.23 = (bf16[256,768]{1,0:T(8,128)(2,1)S(1)}, bf16[256,768]{1,0:T(8,128)(2,1)S(1)}, u32[]{:S(2)}, u32[]{:S(2)}) collective-permute-start(bf16[256,768]{1,0:T(8,128)(2,1)S(1)} %get-tuple-element.121), channel_id=1, source_target_pairs={{0,1},{1,2},{2,3},{4,5},{5,6},{6,7},{8,9},{9,10},{10,11},{12,13},{... | collective-permute-start | bytes 1179656 | tf_op jit(solution)/shard_map/ppermute | solution.py:234
  257.3 11.7 %collective-permute-start.39 = (bf16[256,768]{1,0:T(8,128)(2,1)S(1)}, bf16[256,768]{1,0:T(8,128)(2,1)S(1)}, u32[]{:S(2)}, u32[]{:S(2)}) collective-permute-start(bf16[256,768]{1,0:T(8,128)(2,1)S(1)} %get-tuple-element.84), channel_id=1, source_target_pairs={{1,0},{2,1},{3,2},{5,4},{6,5},{7,6},{9,8},{10,9},{11,10},{13,12},{... | collective-permute-start | bytes 1179656 | tf_op jit(solution)/shard_map/ppermute | solution.py:234
  258.6 13.0 %collective-permute-start.36 = (bf16[256,768]{1,0:T(8,128)(2,1)S(1)}, bf16[256,768]{1,0:T(8,128)(2,1)S(1)}, u32[]{:S(2)}, u32[]{:S(2)}) collective-permute-start(bf16[256,768]{1,0:T(8,128)(2,1)S(1)} %get-tuple-element.84), channel_id=1, source_target_pairs={{0,1},{1,2},{2,3},{4,5},{5,6},{6,7},{8,9},{9,10},{10,11},{12,13},{... | collective-permute-start | bytes 1179656 | tf_op jit(solution)/shard_map/ppermute | solution.py:234
  269.0 14.8 %collective-permute-start.41 = (bf16[256,768]{1,0:T(8,128)(2,1)S(1)}, bf16[256,768]{1,0:T(8,128)(2,1)S(1)}, u32[]{:S(2)}, u32[]{:S(2)}) collective-permute-start(bf16[256,768]{1,0:T(8,128)(2,1)S(1)} %collective-permute-done.39), channel_id=1, source_target_pairs={{2,0},{6,4},{10,8},{14,12},{18,16},{22,20},{26,24},{30,28}} | collective-permute-start | bytes 1179656 | tf_op jit(solution)/shard_map/ppermute | solution.py:234
  270.3 18.3 %collective-permute-start.40 = (bf16[256,768]{1,0:T(8,128)(2,1)S(1)}, bf16[256,768]{1,0:T(8,128)(2,1)S(1)}, u32[]{:S(2)}, u32[]{:S(2)}) collective-permute-start(bf16[256,768]{1,0:T(8,128)(2,1)S(1)} %collective-permute-done.39), channel_id=1, source_target_pairs={{1,0},{2,1},{5,4},{6,5},{9,8},{10,9},{13,12},{14,13},{17,16},{18,1... | collective-permute-start | bytes 1179656 | tf_op jit(solution)/shard_map/ppermute | solution.py:234
  271.6 17.0 %collective-permute-start.38 = (bf16[256,768]{1,0:T(8,128)(2,1)S(1)}, bf16[256,768]{1,0:T(8,128)(2,1)S(1)}, u32[]{:S(2)}, u32[]{:S(2)}) collective-permute-start(bf16[256,768]{1,0:T(8,128)(2,1)S(1)} %collective-permute-done.36), channel_id=1, source_target_pairs={{1,3},{5,7},{9,11},{13,15},{17,19},{21,23},{25,27},{29,31}} | collective-permute-start | bytes 1179656 | tf_op jit(solution)/shard_map/ppermute | solution.py:234
  272.3 16.3 %collective-permute-start.37 = (bf16[256,768]{1,0:T(8,128)(2,1)S(1)}, bf16[256,768]{1,0:T(8,128)(2,1)S(1)}, u32[]{:S(2)}, u32[]{:S(2)}) collective-permute-start(bf16[256,768]{1,0:T(8,128)(2,1)S(1)} %collective-permute-done.36), channel_id=1, source_target_pairs={{2,3},{1,2},{6,7},{5,6},{10,11},{9,10},{14,15},{13,14},{18,19},{17... | collective-permute-start | bytes 1179656 | tf_op jit(solution)/shard_map/ppermute | solution.py:234
  274.8 69.3 %collective-permute-start.63 = (bf16[1152,768]{1,0:T(8,128)(2,1)}, bf16[1152,768]{1,0:T(8,128)(2,1)}, u32[]{:S(2)}, u32[]{:S(2)}) collective-permute-start(bf16[1152,768]{1,0:T(8,128)(2,1)} %constant_dynamic-slice_fusion.4), channel_id=1, source_target_pairs={{0,4},{4,0},{8,12},{12,8},{16,20},{20,16},{24,28},{28,24},{1,5},{5... | collective-permute-start | bytes 5308424 | tf_op jit(solution)/shard_map/ppermute | solution.py:269
  324.0 8.9 %collective-permute-start.50 = (f32[81,128]{1,0:T(8,128)S(1)}, f32[81,128]{1,0:T(8,128)S(1)}, u32[]{:S(2)}, u32[]{:S(2)}) collective-permute-start(f32[81,128]{1,0:T(8,128)S(1)} %bitcast.109), channel_id=1, source_target_pairs={{0,4},{4,0},{8,12},{12,8},{16,20},{20,16},{24,28},{28,24},{1,5},{5... | collective-permute-start | bytes 124424 | tf_op jit(solution)/shard_map/ppermute | solution.py:269
  325.3 45.4 %collective-permute-start.42 = (bf16[256,768]{1,0:T(8,128)(2,1)}, bf16[256,768]{1,0:T(8,128)(2,1)}, u32[]{:S(2)}, u32[]{:S(2)}) collective-permute-start(bf16[256,768]{1,0:T(8,128)(2,1)} %get-tuple-element.110), channel_id=1, source_target_pairs={{3,2},{2,1},{7,6},{6,5},{11,10},{10,9},{15,14},{14,13},{19,18},{18... | collective-permute-start | bytes 1179656 | tf_op jit(solution)/shard_map/ppermute | solution.py:234
  326.7 45.2 %collective-permute-start.46 = (bf16[256,768]{1,0:T(8,128)(2,1)}, bf16[256,768]{1,0:T(8,128)(2,1)}, u32[]{:S(2)}, u32[]{:S(2)}) collective-permute-start(bf16[256,768]{1,0:T(8,128)(2,1)} %get-tuple-element.111), channel_id=1, source_target_pairs={{0,2},{4,6},{8,10},{12,14},{16,18},{20,22},{24,26},{28,30}} | collective-permute-start | bytes 1179656 | tf_op jit(solution)/shard_map/ppermute | solution.py:234
  340.0 47.2 %collective-permute-start.53 = (bf16[1152,768]{1,0:T(8,128)(2,1)}, bf16[1152,768]{1,0:T(8,128)(2,1)}, u32[]{:S(2)}, u32[]{:S(2)}) collective-permute-start(bf16[1152,768]{1,0:T(8,128)(2,1)} %constant_dynamic-slice_fusion.9), channel_id=1, source_target_pairs={{0,4},{4,0},{8,12},{12,8},{16,20},{20,16},{24,28},{28,24},{1,5},{5... | collective-permute-start | bytes 5308424 | tf_op jit(solution)/shard_map/ppermute | solution.py:269
  346.2 11.5 %collective-permute-start.68 = (bf16[288,768]{1,0:T(8,128)(2,1)S(1)}, bf16[288,768]{1,0:T(8,128)(2,1)S(1)}, u32[]{:S(2)}, u32[]{:S(2)}) collective-permute-start(bf16[288,768]{1,0:T(8,128)(2,1)S(1)} %constant_dynamic-slice_fusion.1), channel_id=1, source_target_pairs={{0,16},{4,20},{8,24},{12,28},{16,0},{20,4},{24,8},{28,12},{1,17},{... | collective-permute-start | bytes 1327112 | tf_op jit(solution)/shard_map/ppermute | solution.py:269
  348.5 10.9 %collective-permute-start.64 = (bf16[288,768]{1,0:T(8,128)(2,1)S(1)}, bf16[288,768]{1,0:T(8,128)(2,1)S(1)}, u32[]{:S(2)}, u32[]{:S(2)}) collective-permute-start(bf16[288,768]{1,0:T(8,128)(2,1)S(1)} %constant_dynamic-slice_fusion.3), channel_id=1, source_target_pairs={{0,8},{4,12},{8,0},{12,4},{16,24},{20,28},{24,16},{28,20},{1,9},{5... | collective-permute-start | bytes 1327112 | tf_op jit(solution)/shard_map/ppermute | solution.py:269
  366.1 7.1 %collective-permute-start.45 = (bf16[256,768]{1,0:T(8,128)(2,1)S(1)}, bf16[256,768]{1,0:T(8,128)(2,1)S(1)}, u32[]{:S(2)}, u32[]{:S(2)}) collective-permute-start(bf16[256,768]{1,0:T(8,128)(2,1)S(1)} %copy-done.43), channel_id=1, source_target_pairs={{0,1},{1,2},{4,5},{5,6},{8,9},{9,10},{12,13},{13,14},{16,17},{17,1... | collective-permute-start | bytes 1179656 | tf_op jit(solution)/shard_map/ppermute | solution.py:234
  370.7 14.1 %collective-permute-start.66 = (bf16[144,768]{1,0:T(8,128)(2,1)S(1)}, bf16[144,768]{1,0:T(8,128)(2,1)S(1)}, u32[]{:S(2)}, u32[]{:S(2)}) collective-permute-start(bf16[144,768]{1,0:T(8,128)(2,1)S(1)} %add_convert_fusion.19), channel_id=1, source_target_pairs={{0,16},{4,20},{8,24},{12,28},{16,0},{20,4},{24,8},{28,12},{1,17},{... | collective-permute-start | bytes 663560 | tf_op jit(solution)/shard_map/ppermute | solution.py:269
  371.9 15.1 %collective-permute-start.71 = (bf16[288,768]{1,0:T(8,128)(2,1)S(1)}, bf16[288,768]{1,0:T(8,128)(2,1)S(1)}, u32[]{:S(2)}, u32[]{:S(2)}) collective-permute-start(bf16[288,768]{1,0:T(8,128)(2,1)S(1)} %pad_maximum_fusion.13), channel_id=1, source_target_pairs={{0,16},{4,20},{8,24},{12,28},{16,0},{20,4},{24,8},{28,12},{1,17},{... | collective-permute-start | bytes 1327112 | tf_op jit(solution)/shard_map/ppermute | solution.py:269
  374.5 50.6 %collective-permute-start.44 = (bf16[256,768]{1,0:T(8,128)(2,1)S(1)}, bf16[256,768]{1,0:T(8,128)(2,1)S(1)}, u32[]{:S(2)}, u32[]{:S(2)}) collective-permute-start(bf16[256,768]{1,0:T(8,128)(2,1)S(1)} %get-tuple-element.108), channel_id=1, source_target_pairs={{1,0},{2,1},{3,2},{5,4},{6,5},{7,6},{9,8},{10,9},{11,10},{13,12},{... | collective-permute-start | bytes 1179656 | tf_op jit(solution)/shard_map/ppermute | solution.py:234
  375.9 49.2 %collective-permute-start.47 = (bf16[256,768]{1,0:T(8,128)(2,1)S(1)}, bf16[256,768]{1,0:T(8,128)(2,1)S(1)}, u32[]{:S(2)}, u32[]{:S(2)}) collective-permute-start(bf16[256,768]{1,0:T(8,128)(2,1)S(1)} %get-tuple-element.109), channel_id=1, source_target_pairs={{0,1},{1,2},{2,3},{4,5},{5,6},{6,7},{8,9},{9,10},{10,11},{12,13},{... | collective-permute-start | bytes 1179656 | tf_op jit(solution)/shard_map/ppermute | solution.py:234
  384.9 11.9 %collective-permute-start.67 = (bf16[288,768]{1,0:T(8,128)(2,1)S(1)}, bf16[288,768]{1,0:T(8,128)(2,1)S(1)}, u32[]{:S(2)}, u32[]{:S(2)}) collective-permute-start(bf16[288,768]{1,0:T(8,128)(2,1)S(1)} %pad_maximum_fusion.12), channel_id=1, source_target_pairs={{0,8},{4,12},{8,0},{12,4},{16,24},{20,28},{24,16},{28,20},{1,9},{5... | collective-permute-start | bytes 1327112 | tf_op jit(solution)/shard_map/ppermute | solution.py:269
  389.3 10.4 %collective-permute-start.58 = (bf16[288,768]{1,0:T(8,128)(2,1)S(1)}, bf16[288,768]{1,0:T(8,128)(2,1)S(1)}, u32[]{:S(2)}, u32[]{:S(2)}) collective-permute-start(bf16[288,768]{1,0:T(8,128)(2,1)S(1)} %constant_dynamic-slice_fusion.6), channel_id=1, source_target_pairs={{0,16},{4,20},{8,24},{12,28},{16,0},{20,4},{24,8},{28,12},{1,17},{... | collective-permute-start | bytes 1327112 | tf_op jit(solution)/shard_map/ppermute | solution.py:269
  397.0 11.2 %collective-permute-start.54 = (bf16[288,768]{1,0:T(8,128)(2,1)S(1)}, bf16[288,768]{1,0:T(8,128)(2,1)S(1)}, u32[]{:S(2)}, u32[]{:S(2)}) collective-permute-start(bf16[288,768]{1,0:T(8,128)(2,1)S(1)} %constant_dynamic-slice_fusion.8), channel_id=1, source_target_pairs={{0,8},{4,12},{8,0},{12,4},{16,24},{20,28},{24,16},{28,20},{1,9},{5... | collective-permute-start | bytes 1327112 | tf_op jit(solution)/shard_map/ppermute | solution.py:269
  399.7 34.4 %collective-permute-start.72 = (bf16[1152,768]{1,0:T(8,128)(2,1)S(1)}, bf16[1152,768]{1,0:T(8,128)(2,1)S(1)}, u32[]{:S(2)}, u32[]{:S(2)}) collective-permute-start(bf16[1152,768]{1,0:T(8,128)(2,1)S(1)} %pad_maximum_fusion.5), channel_id=1, source_target_pairs={{0,4},{4,0},{8,12},{12,8},{16,20},{20,16},{24,28},{28,24},{1,5},{5... | collective-permute-start | bytes 5308424 | tf_op jit(solution)/shard_map/ppermute | solution.py:269
  399.9 11.7 %collective-permute-start.59 = (bf16[144,768]{1,0:T(8,128)(2,1)S(1)}, bf16[144,768]{1,0:T(8,128)(2,1)S(1)}, u32[]{:S(2)}, u32[]{:S(2)}) collective-permute-start(bf16[144,768]{1,0:T(8,128)(2,1)S(1)} %constant_dynamic-slice_fusion.5), channel_id=1, source_target_pairs={{0,8},{4,12},{8,0},{12,4},{16,24},{20,28},{24,16},{28,20},{1,9},{5... | collective-permute-start | bytes 663560 | tf_op jit(solution)/shard_map/ppermute | solution.py:269
  408.4 7.3 %collective-permute-start.55 = (bf16[144,768]{1,0:T(8,128)(2,1)S(1)}, bf16[144,768]{1,0:T(8,128)(2,1)S(1)}, u32[]{:S(2)}, u32[]{:S(2)}) collective-permute-start(bf16[144,768]{1,0:T(8,128)(2,1)S(1)} %constant_dynamic-slice_fusion.7), channel_id=1, source_target_pairs={{0,16},{4,20},{8,24},{12,28},{16,0},{20,4},{24,8},{28,12},{1,17},{... | collective-permute-start | bytes 663560 | tf_op jit(solution)/shard_map/ppermute | solution.py:269
  411.7 7.5 %collective-permute-start.60 = (bf16[144,768]{1,0:T(8,128)(2,1)S(1)}, bf16[144,768]{1,0:T(8,128)(2,1)S(1)}, u32[]{:S(2)}, u32[]{:S(2)}) collective-permute-start(bf16[144,768]{1,0:T(8,128)(2,1)S(1)} %add_convert_fusion.20), channel_id=1, source_target_pairs={{0,8},{4,12},{8,0},{12,4},{16,24},{20,28},{24,16},{28,20},{1,9},{5... | collective-permute-start | bytes 663560 | tf_op jit(solution)/shard_map/ppermute | solution.py:269
  415.7 7.3 %collective-permute-start.56 = (bf16[144,768]{1,0:T(8,128)(2,1)S(1)}, bf16[144,768]{1,0:T(8,128)(2,1)S(1)}, u32[]{:S(2)}, u32[]{:S(2)}) collective-permute-start(bf16[144,768]{1,0:T(8,128)(2,1)S(1)} %add_convert_fusion.21), channel_id=1, source_target_pairs={{0,16},{4,20},{8,24},{12,28},{16,0},{20,4},{24,8},{28,12},{1,17},{... | collective-permute-start | bytes 663560 | tf_op jit(solution)/shard_map/ppermute | solution.py:269
  419.3 8.5 %collective-permute-start.61 = (bf16[288,768]{1,0:T(8,128)(2,1)S(1)}, bf16[288,768]{1,0:T(8,128)(2,1)S(1)}, u32[]{:S(2)}, u32[]{:S(2)}) collective-permute-start(bf16[288,768]{1,0:T(8,128)(2,1)S(1)} %pad_maximum_fusion.11), channel_id=1, source_target_pairs={{0,16},{4,20},{8,24},{12,28},{16,0},{20,4},{24,8},{28,12},{1,17},{... | collective-permute-start | bytes 1327112 | tf_op jit(solution)/shard_map/ppermute | solution.py:269
  423.1 8.4 %collective-permute-start.57 = (bf16[288,768]{1,0:T(8,128)(2,1)S(1)}, bf16[288,768]{1,0:T(8,128)(2,1)S(1)}, u32[]{:S(2)}, u32[]{:S(2)}) collective-permute-start(bf16[288,768]{1,0:T(8,128)(2,1)S(1)} %pad_maximum_fusion.10), channel_id=1, source_target_pairs={{0,8},{4,12},{8,0},{12,4},{16,24},{20,28},{24,16},{28,20},{1,9},{5... | collective-permute-start | bytes 1327112 | tf_op jit(solution)/shard_map/ppermute | solution.py:269
  (69 other events, 704.3 us)
